TPU v7x, 256 devices: a whole 4x4x8 slice. The times are simulated.
256 devices in a mesh: fine: 32 (over x, z), coarse: 8 (over y, core).
Axes of the slice: x: 4, y: 4, z: 8, core: 2. Of those that a mesh axis runs over, the one named last changes fastest.
Arguments:
- fine_blocks: float32 [7, 10, 10, 131072], P(None, None, None, ('fine', 'coarse')), may hold values from -0.035 to 0.835
- fine_columns: int32 [7, 131072], P(None, ('fine', 'coarse')), may hold values from 0 to 1279, as said below
- coarse_slots: int32 [7, 131072], P(None, ('fine', 'coarse')), may hold values from 0 to 6, as said below
- ghost_lists: int32 [196608], P(('fine', 'coarse')), may hold values from 0 to 511, as said below
- tentative: float32 [10, 10, 131072], P(None, None, ('fine', 'coarse')), may hold values from -0.05 to 1.05
- members: int32 [15, 16384], P(None, ('fine', 'coarse')), may hold values from -1 to 511, as said below
- coarse_columns: int32 [7, 16384], P(None, ('fine', 'coarse')), may hold values from 0 to 191, as said below
- coarse_rhs: float32 [10, 16384], P(None, ('fine', 'coarse')), may hold values from -6 to 6
- coarse_guess: float32 [10, 16384], P(None, ('fine', 'coarse')), may hold values from -6 to 6
Outputs:
- coarse_op: float32 [7, 10, 10, 16384], P(None, None, None, ('fine', 'coarse'))
- coarse_iterate: float32 [10, 16384], P(None, ('fine', 'coarse'))
Inputs may be any that keep to these rules, and one draw needn't show every extreme that they name: `fine_columns`: in block g, values below 512 are the block's own cells, 512 + p is the p-th listed cell of block g-1 and 896 + p the p-th listed cell of block g+1; row 0 names the cell itself; the first block never reads block g-1 and the last never block g+1; the cell named lies in the aggregate that coarse_columns names for the coarse block of coarse_slots. `coarse_slots`: row 0 is 0 and every other row lies in 1 to 6. `ghost_lists`: each half of a block's 384 * 2 values lists distinct cells of the neighbouring block, local to it. `members`: the lists of a block's aggregates hold each of its cells exactly once, filled from the top and padded with -1; every block has an aggregate of 15 cells and one of 1 cell. `coarse_columns`: row 0 names the row's own aggregate and no other row does; the first block names no aggregate of block g-1, the last none of block g+1.
All inputs are finite; a program needn't handle non-finite values.
Results may differ from a plain program's by a relative error of at most 0.0003.
Values sent between devices are 32-bit elements; how exact they have to be, the bound alone decides.
A program may use at most 64 MiB of HBM per device.

v0:
```python
import jax
import jax.numpy as jnp
from jax import lax
from jax.sharding import PartitionSpec as P

SWEEPS = 2


def with_halo(block, sides, width):
    for axis, dim in sides:
        count = lax.axis_size(axis)
        forward = [(i, i + 1) for i in range(count - 1)]
        backward = [(target, source) for source, target in forward]
        low = lax.ppermute(
            lax.slice_in_dim(block, block.shape[dim] - width, None, axis=dim), axis, forward
        )
        high = lax.ppermute(lax.slice_in_dim(block, 0, width, axis=dim), axis, backward)
        block = jnp.concatenate([low, block, high], axis=dim)
    return block


def invert_blocks(diagonal):
    block_order = diagonal.shape[0]
    identity = jnp.broadcast_to(
        jnp.eye(block_order, dtype=diagonal.dtype)[:, :, None], diagonal.shape
    )
    tableau = jnp.concatenate([diagonal, identity], axis=1)
    for pivot_row in range(block_order):
        scaled = tableau[pivot_row] / tableau[pivot_row, pivot_row][None, :]
        tableau = tableau - tableau[:, pivot_row][:, None, :] * scaled[None]
        tableau = tableau.at[pivot_row].set(scaled)
    return tableau[:, block_order:]


def gather_cells(blocks, index):
    lead = blocks.shape[:-1]
    flat = blocks.reshape(-1, blocks.shape[-1])
    taken = jnp.take(flat, index.reshape(-1), axis=1)
    return taken.reshape(lead + index.shape)


def block_product(left, right):
    total = None
    for inner in range(left.shape[2]):
        term = left[:, :, inner, None, :] * jnp.swapaxes(right[inner], 0, 1)[:, None, :, :]
        total = term if total is None else total + term
    return total


def transposed_product(basis, blocks):
    total = None
    for inner in range(basis.shape[0]):
        term = basis[inner][None, :, None, :] * blocks[:, inner][:, None, :, :]
        total = term if total is None else total + term
    return total


def body(
    fine_blocks,
    fine_columns,
    coarse_slots,
    ghost_lists,
    tentative,
    members,
    coarse_columns,
    coarse_rhs,
    coarse_guess,
):
    ghost_count = ghost_lists.shape[0] // 2
    agg_count = members.shape[1]
    wanted = with_halo(ghost_lists, ((("fine", "coarse"), 0),), ghost_count)
    wanted_rows = jnp.concatenate([wanted[:ghost_count], wanted[3 * ghost_count :]], axis=0)
    packed = gather_cells(tentative, wanted_rows)
    arrived = with_halo(packed, ((("fine", "coarse"), 2),), ghost_count)
    from_prev = arrived[:, :, :ghost_count]
    from_next = arrived[:, :, 3 * ghost_count :]
    extended = jnp.concatenate([tentative, from_prev, from_next], axis=2)
    picked_basis = gather_cells(extended, fine_columns)
    ap_blocks = block_product(fine_blocks, picked_basis)
    product = transposed_product(tentative, ap_blocks)
    slot_count = coarse_columns.shape[0]
    slot_range = jnp.arange(slot_count, dtype=jnp.int32)
    per_slot = None
    for entry in range(coarse_slots.shape[0]):
        onehot = (coarse_slots[entry][None, :] == slot_range[:, None]).astype(jnp.float32)
        term = onehot[:, None, None, :] * product[entry][None]
        per_slot = term if per_slot is None else per_slot + term
    weight = (members >= 0).astype(jnp.float32)
    gathered = gather_cells(per_slot, jnp.maximum(members, 0))
    coarse_op = jnp.sum(gathered * weight, axis=3)
    inverse = invert_blocks(coarse_op[0])
    iterate = coarse_guess
    for sweep in range(SWEEPS):
        wide_iterate = with_halo(iterate, ((("fine", "coarse"), 1),), agg_count)
        neighbours = jnp.take(wide_iterate, coarse_columns.reshape(-1), axis=1).reshape(
            iterate.shape[0], slot_count, agg_count
        )
        applied = jnp.sum(coarse_op * jnp.swapaxes(neighbours, 0, 1)[:, None, :, :], axis=(0, 2))
        update = jnp.sum(inverse * (coarse_rhs - applied)[None, :, :], axis=1)
        iterate = iterate + update
    return (coarse_op, iterate)


def solution(mesh):
    placed = (
        P(None, None, None, ("fine", "coarse")),
        P(None, ("fine", "coarse")),
        P(None, ("fine", "coarse")),
        P(("fine", "coarse")),
        P(None, None, ("fine", "coarse")),
        P(None, ("fine", "coarse")),
        P(None, ("fine", "coarse")),
        P(None, ("fine", "coarse")),
        P(None, ("fine", "coarse")),
    )
    return jax.shard_map(
        body,
        mesh=mesh,
        in_specs=placed,
        out_specs=(P(None, None, None, ("fine", "coarse")), P(None, ("fine", "coarse"))),
        check_vma=False,
    )
```

profile of v0, /device:TPU:6, one launch (start us, length us, event | category | flops | bytes accessed | tf_op | source)
XLA Modules:
  0.0 128.9 jit_solution(1239199218297122955)
XLA Ops:
  0.7 2.1 %collective-permute-start.4 = (f32[10,64]{1,0:T(8,128)}, f32[10,64]{1,0:T(8,128)S(1)}, u32[]{:S(2)}, u32[]{:S(2)}) collective-permute-start(f32[10,64]{1,0:T(8,128)} %param.39), channel_id=1, source_target_pairs={{0,1},{1,2},{2,3},{3,4},{4,5},{5,6},{6,7},{7,8},{8,9},{9,10},{10,1... | collective-permute-start | bytes 7688 | tf_op jit(solution)/shard_map/ppermute | solution.py:14
  2.7 9.9 %collective-permute-start.5 = (f32[10,64]{1,0:T(8,128)}, f32[10,64]{1,0:T(8,128)S(1)}, u32[]{:S(2)}, u32[]{:S(2)}) collective-permute-start(f32[10,64]{1,0:T(8,128)} %param.39), channel_id=1, source_target_pairs={{1,0},{2,1},{3,2},{4,3},{5,4},{6,5},{7,6},{8,7},{9,8},{10,9},{11,1... | collective-permute-start | bytes 7688 | tf_op jit(solution)/shard_map/ppermute | solution.py:17
  12.6 0.8 fusion.35
  13.4 1.9 %collective-permute-start = (s32[384]{0:T(512)S(1)}, s32[384]{0:T(512)S(1)}, u32[]{:S(2)}, u32[]{:S(2)}) collective-permute-start(s32[384]{0:T(512)S(1)} %get-tuple-element.188), channel_id=1, source_target_pairs={{0,1},{1,2},{2,3},{3,4},{4,5},{5,6},{6,7},{7,8},{8,9},{9,10},{10,1... | collective-permute-start | bytes 4616 | tf_op jit(solution)/shard_map/ppermute | solution.py:14
  15.3 7.9 %collective-permute-start.1 = (s32[384]{0:T(512)S(1)}, s32[384]{0:T(512)S(1)}, u32[]{:S(2)}, u32[]{:S(2)}) collective-permute-start(s32[384]{0:T(512)S(1)} %get-tuple-element.187), channel_id=1, source_target_pairs={{1,0},{2,1},{3,2},{4,3},{5,4},{6,5},{7,6},{8,7},{9,8},{10,9},{11,1... | collective-permute-start | bytes 4616 | tf_op jit(solution)/shard_map/ppermute | solution.py:17
  23.2 0.7 broadcast_maximum_fusion
  23.9 1.3 %broadcast_compare_fusion = (pred[15,64]{1,0:T(8,128)(4,1)}, f32[15,64]{1,0:T(8,128)S(1)}) fusion(s32[15,64]{1,0:T(8,128)} %param.36), kind=kLoop, calls=%fused_computation.125 | loop fusion | flops 3840 | bytes 8640 | tf_op jit(solution)/shard_map/jit(_take)/le | solution.py:38
  25.2 0.6 fusion.11
  25.8 0.8 reshape.827
  26.7 0.7 reshape.822
  27.4 0.7 copy.84
  28.2 2.7 %slice_bitcast_fusion.26 = (f32[7,10,512]{2,0,1:T(8,128)}, f32[7,10,512]{2,0,1:T(8,128)}, f32[7,10,512]{2,0,1:T(8,128)}, f32[7,10,512]{2,0,1:T(8,128)}, f32[7,10...) fusion(f32[7,10,10,512]{3,0,2,1:T(8,128)} %param.31), kind=kLoop, calls=%fused_computation.42 | loop fusion | bytes 2867200 | tf_op jit(solution)/shard_map/mul | solution.py:45
  30.9 0.7 slice_bitcast_fusion.37
  31.7 0.6 fusion.1
  32.3 0.6 fusion.3
  32.9 0.6 fusion.5
  34.3 1.6 %gather_fusion = f32[768,100]{1,0:T(8,128)S(1)} fusion(f32[100,512]{0,1:T(8,128)S(1)} %copy.54, s32[1024]{0:T(1024)S(1)} %get-tuple-element.190), kind=kCustom, calls=%fused_computation.2 | custom fusion | bytes 617472 | tf_op jit(solution)/shard_map/jit(_take)/gather | solution.py:38
  36.3 1.9 %collective-permute-start.2 = (f32[10,10,384]{2,1,0:T(8,128)S(1)}, f32[10,10,384]{2,1,0:T(8,128)S(1)}, u32[]{:S(2)}, u32[]{:S(2)}) collective-permute-start(f32[10,10,384]{2,1,0:T(8,128)S(1)} %get-tuple-element.166), channel_id=1, source_target_pairs={{0,1},{1,2},{2,3},{3,4},{4,5},{5,6},{6,7},{7,8},{8,9},{9,10},{10,1... | collective-permute-start | bytes 460808 | tf_op jit(solution)/shard_map/ppermute | solution.py:14
  38.2 7.9 %collective-permute-start.3 = (f32[10,10,384]{2,1,0:T(8,128)S(1)}, f32[10,10,384]{2,1,0:T(8,128)S(1)}, u32[]{:S(2)}, u32[]{:S(2)}) collective-permute-start(f32[10,10,384]{2,1,0:T(8,128)S(1)} %get-tuple-element.167), channel_id=1, source_target_pairs={{1,0},{2,1},{3,2},{4,3},{5,4},{6,5},{7,6},{8,7},{9,8},{10,9},{11,1... | collective-permute-start | bytes 460808 | tf_op jit(solution)/shard_map/ppermute | solution.py:17
  46.3 1.2 gather_fusion.3
  48.0 1.8 %collective-permute-done.3 = f32[10,10,384]{2,1,0:T(8,128)S(1)} collective-permute-done((f32[10,10,384]{2,1,0:T(8,128)S(1)}, f32[10,10,384]{2,1,0:T(8,128)S(1)}, u32[]{:S(2)}, u32[]{:S(2)}) %collective-permute-start.3) | collective-permute-done | bytes 153632 | tf_op jit(solution)/shard_map/ppermute | solution.py:17
  50.2 5.7 %gather_fusion.1 = f32[3584,100]{1,0:T(8,128)S(1)} fusion(f32[100,1280]{0,1:T(8,128)S(1)} %copy.56, s32[4096]{0:T(1024)S(1)} %pad_clamp_fusion), kind=kCustom, calls=%fused_computation.3 | custom fusion | bytes 2881536 | tf_op jit(solution)/shard_map/jit(_take)/gather | solution.py:38
  55.9 1.8 %select_bitcast_fusion = f32[100,3584]{0,1:T(8,128)S(1)} fusion(f32[3584,100]{1,0:T(8,128)S(1)} %gather_fusion.1, pred[3584]{0:T(1024)(128)(4,1)S(1)} %compare_and_fusion), kind=kLoop, calls=%fused_computation.9 | loop fusion | flops 358400 | bytes 2870784 | tf_op jit(solution)/shard_map/jit(_take)/select_n | solution.py:38
  57.7 8.0 %fusion.32 = (f32[10,3584]{0,1:T(8,128)}, f32[10,3584]{0,1:T(8,128)S(1)}, f32[10,3584]{0,1:T(8,128)}, f32[10,3584]{0,1:T(8,128)}, f32[10,3584]{0,1:T(8,128)}, /*...) fusion(f32[100,3584]{0,1:T(8,128)S(1)} %select_bitcast_fusion), kind=kLoop, calls=%fused_computation.160 | loop fusion | bytes 2867200 | tf_op jit(solution)/shard_map/slice | solution.py:45
  65.7 2.0 %copy.57 = f32[7,10,512]{2,1,0:T(8,128)S(1)} copy(f32[7,10,512]{1,2,0:T(8,128)} %bitcast.212) | data formatting | bytes 286720 | tf_op jit(solution)/shard_map/transpose | solution.py:45
  67.8 2.1 %copy.58 = f32[7,10,512]{2,1,0:T(8,128)S(1)} copy(f32[7,10,512]{1,2,0:T(8,128)} %bitcast.211) | data formatting | bytes 286720 | tf_op jit(solution)/shard_map/transpose | solution.py:45
  69.8 2.1 %copy.59 = f32[7,10,512]{2,1,0:T(8,128)S(1)} copy(f32[7,10,512]{1,2,0:T(8,128)} %bitcast.210) | data formatting | bytes 286720 | tf_op jit(solution)/shard_map/transpose | solution.py:45
  71.9 2.1 %copy.60 = f32[7,10,512]{2,1,0:T(8,128)S(1)} copy(f32[7,10,512]{1,2,0:T(8,128)} %bitcast.209) | data formatting | bytes 286720 | tf_op jit(solution)/shard_map/transpose | solution.py:45
  73.9 2.1 %copy.61 = f32[7,10,512]{2,1,0:T(8,128)S(1)} copy(f32[7,10,512]{1,2,0:T(8,128)} %bitcast.208) | data formatting | bytes 286720 | tf_op jit(solution)/shard_map/transpose | solution.py:45
  76.0 2.1 %copy.62 = f32[7,10,512]{2,1,0:T(8,128)S(1)} copy(f32[7,10,512]{1,2,0:T(8,128)} %bitcast.207) | data formatting | bytes 286720 | tf_op jit(solution)/shard_map/transpose | solution.py:45
  78.0 2.1 %copy.63 = f32[7,10,512]{2,1,0:T(8,128)S(1)} copy(f32[7,10,512]{1,2,0:T(8,128)} %bitcast.206) | data formatting | bytes 286720 | tf_op jit(solution)/shard_map/transpose | solution.py:45
  80.1 2.7 %copy.64 = f32[7,10,512]{2,1,0:T(8,128)} copy(f32[7,10,512]{1,2,0:T(8,128)} %bitcast.205) | data formatting | bytes 286720 | tf_op jit(solution)/shard_map/transpose | solution.py:45
  82.8 2.7 %copy.65 = f32[7,10,512]{2,1,0:T(8,128)} copy(f32[7,10,512]{1,2,0:T(8,128)} %bitcast.204) | data formatting | bytes 286720 | tf_op jit(solution)/shard_map/transpose | solution.py:45
  85.6 1.2 copy.66
  86.8 3.0 %multiply_add_fusion.1 = f32[7,10,10,512]{3,2,0,1:T(8,128)S(1)} fusion(f32[7,10,512]{2,1,0:T(8,128)} %copy.66, f32[7,10,512]{2,0,1:T(8,128)} %get-tuple-element.164, f32[7,10,512]{2,1,0:T(8,128)} %copy.65, f32[7,10,512]{2,0,1:T(8,128)} %get-tuple-element.165, f32[7,10,512]{2,1,0:T(8,128)} %copy.64, f32[7,10,512]{2,0,1:T(8,128)} %get-tuple-element.157, ...), kind=kLoop, calls=%fused_computation.8 | loop fusion | flops 6809600 | bytes 4300800 | tf_op jit(solution)/shard_map/add | solution.py:46
  90.7 2.0 %multiply_add_fusion = f32[7,10,10,512]{3,2,1,0:T(8,128)S(1)} fusion(f32[7,10,512]{2,1,0:T(8,128)S(1)} %get-tuple-element.137, f32[10,512]{1,0:T(8,128)S(1)} %copy-done.8, f32[7,10,512]{2,1,0:T(8,128)S(1)} %get-tuple-element.138, f32[10,512]{1,0:T(8,128)S(1)} %copy-done.9, f32[7,10,512]{2,1,0:T(8,128)S(1)} %get-tuple-element.139, f32[10,512]{1,0:T(8,128)S(1)} %copy-done.1, ...), kind=kLoop, calls=%fused_computation.7 | loop fusion | flops 6809600 | bytes 3072000 | tf_op jit(solution)/shard_map/add | solution.py:54
  93.5 1.0 add_add_fusion
  94.5 1.3 %reshape.832 = f32[700,512]{1,0:T(8,128)} reshape(f32[7,10,10,512]{3,2,1,0:T(8,128)S(1)} %add_add_fusion) | data formatting | bytes 2867200 | tf_op jit(solution)/shard_map/add | solution.py:87
  95.9 1.8 %copy.67 = f32[700,512]{0,1:T(8,128)S(1)} copy(f32[700,512]{1,0:T(8,128)} %reshape.832) | data formatting | bytes 2867200 | tf_op jit(solution)/shard_map/add | solution.py:87
  97.7 5.4 %gather_fusion.2 = f32[960,700]{1,0:T(8,128)} fusion(f32[700,512]{0,1:T(8,128)S(1)} %copy.67, s32[1024]{0:T(1024)S(1)} %copy-done.22), kind=kCustom, calls=%fused_computation.4 | custom fusion | bytes 5379840 | tf_op jit(solution)/shard_map/jit(_take)/gather | solution.py:38
  103.1 2.6 %copy.68 = f32[700,960]{1,0:T(8,128)S(1)} copy(f32[700,960]{0,1:T(8,128)} %bitcast.202) | data formatting | bytes 5376000 | tf_op jit(solution)/shard_map/jit(_take)/gather | solution.py:38
  105.7 4.1 %gather.23 = f32[7,10,10,15,64]{4,3,2,1,0:T(8,128)} reshape(f32[700,960]{1,0:T(8,128)S(1)} %copy.68) | data formatting | bytes 5376000 | tf_op jit(solution)/shard_map/jit(_take)/gather | solution.py:38
  109.8 4.2 %multiply_reduce_fusion = f32[7,10,10,64]{3,2,1,0:T(8,128)S(1)} fusion(f32[7,10,10,15,64]{4,3,2,1,0:T(8,128)} %gather.23, f32[15,64]{1,0:T(8,128)S(1)} %get-tuple-element.186, pred[15,64]{1,0:T(8,128)(4,1)S(1)} %copy-done.24), kind=kLoop, calls=%fused_computation.5 | loop fusion | flops 1971200 | bytes 2872000 | tf_op jit(solution)/shard_map/reduce_sum | solution.py:90
  115.2 1.9 %collective-permute-start.6 = (f32[10,64]{1,0:T(8,128)S(1)}, f32[10,64]{1,0:T(8,128)S(1)}, u32[]{:S(2)}, u32[]{:S(2)}) collective-permute-start(f32[10,64]{1,0:T(8,128)S(1)} %add.210), channel_id=1, source_target_pairs={{0,1},{1,2},{2,3},{3,4},{4,5},{5,6},{6,7},{7,8},{8,9},{9,10},{10,1... | collective-permute-start | bytes 7688 | tf_op jit(solution)/shard_map/ppermute | solution.py:14
  117.1 8.0 %collective-permute-start.7 = (f32[10,64]{1,0:T(8,128)S(1)}, f32[10,64]{1,0:T(8,128)S(1)}, u32[]{:S(2)}, u32[]{:S(2)}) collective-permute-start(f32[10,64]{1,0:T(8,128)S(1)} %add.210), channel_id=1, source_target_pairs={{1,0},{2,1},{3,2},{4,3},{5,4},{6,5},{7,6},{8,7},{9,8},{10,9},{11,1... | collective-permute-start | bytes 7688 | tf_op jit(solution)/shard_map/ppermute | solution.py:17
  125.2 1.0 copy.73
  126.7 1.2 gather_fusion.4
  128.3 0.6 add.211
  (167 shorter events, 5.6 us)
Async XLA Ops:
  0.6 30.3 %copy-start = (f32[10,10,512]{2,1,0:T(8,128)S(1)}, f32[10,10,512]{2,1,0:T(8,128)}, u32[]{:S(2)}) copy-start(f32[10,10,512]{2,1,0:T(8,128)} %param.35) | copy-start | bytes 614404
  0.6 31.0 %copy-start.23 = (s32[7,512]{1,0:T(8,128)S(1)}, s32[7,512]{1,0:T(8,128)}, u32[]{:S(2)}) copy-start(s32[7,512]{1,0:T(8,128)} %param.33) | copy-start | bytes 43012
  0.7 45.4 %collective-permute-start.4 = (f32[10,64]{1,0:T(8,128)}, f32[10,64]{1,0:T(8,128)S(1)}, u32[]{:S(2)}, u32[]{:S(2)}) collective-permute-start(f32[10,64]{1,0:T(8,128)} %param.39), channel_id=1, source_target_pairs={{0,1},{1,2},{2,3},{3,4},{4,5},{5,6},{6,7},{7,8},{8,9},{9,10},{10,1... | collective-permute-start | bytes 7688 | tf_op jit(solution)/shard_map/ppermute | solution.py:14
  2.7 43.4 %collective-permute-start.5 = (f32[10,64]{1,0:T(8,128)}, f32[10,64]{1,0:T(8,128)S(1)}, u32[]{:S(2)}, u32[]{:S(2)}) collective-permute-start(f32[10,64]{1,0:T(8,128)} %param.39), channel_id=1, source_target_pairs={{1,0},{2,1},{3,2},{4,3},{5,4},{6,5},{7,6},{8,7},{9,8},{10,9},{11,1... | collective-permute-start | bytes 7688 | tf_op jit(solution)/shard_map/ppermute | solution.py:17
  13.4 20.3 %collective-permute-start = (s32[384]{0:T(512)S(1)}, s32[384]{0:T(512)S(1)}, u32[]{:S(2)}, u32[]{:S(2)}) collective-permute-start(s32[384]{0:T(512)S(1)} %get-tuple-element.188), channel_id=1, source_target_pairs={{0,1},{1,2},{2,3},{3,4},{4,5},{5,6},{6,7},{7,8},{8,9},{9,10},{10,1... | collective-permute-start | bytes 4616 | tf_op jit(solution)/shard_map/ppermute | solution.py:14
  15.3 18.4 %collective-permute-start.1 = (s32[384]{0:T(512)S(1)}, s32[384]{0:T(512)S(1)}, u32[]{:S(2)}, u32[]{:S(2)}) collective-permute-start(s32[384]{0:T(512)S(1)} %get-tuple-element.187), channel_id=1, source_target_pairs={{1,0},{2,1},{3,2},{4,3},{5,4},{6,5},{7,6},{8,7},{9,8},{10,9},{11,1... | collective-permute-start | bytes 4616 | tf_op jit(solution)/shard_map/ppermute | solution.py:17
  26.6 20.9 %copy-start.25 = (pred[448]{0:T(512)(128)(4,1)}, pred[448]{0:T(512)(128)(4,1)S(1)}, u32[]{:S(2)}) copy-start(pred[448]{0:T(512)(128)(4,1)S(1)} %compare_and_fusion.2) | copy-start | bytes 1348
  33.5 12.8 %copy-start.20 = (s32[1024]{0:T(1024)}, s32[1024]{0:T(1024)S(1)}, u32[]{:S(2)}) copy-start(s32[1024]{0:T(1024)S(1)} %pad_clamp_fusion.1) | copy-start | bytes 12292
  35.9 10.2 %copy-start.16 = (f32[10,64]{1,0:T(8,128)S(1)}, f32[10,64]{1,0:T(8,128)}, u32[]{:S(2)}) copy-start(f32[10,64]{1,0:T(8,128)} %param.39) | copy-start | bytes 7684
  36.3 11.7 %collective-permute-start.2 = (f32[10,10,384]{2,1,0:T(8,128)S(1)}, f32[10,10,384]{2,1,0:T(8,128)S(1)}, u32[]{:S(2)}, u32[]{:S(2)}) collective-permute-start(f32[10,10,384]{2,1,0:T(8,128)S(1)} %get-tuple-element.166), channel_id=1, source_target_pairs={{0,1},{1,2},{2,3},{3,4},{4,5},{5,6},{6,7},{7,8},{8,9},{9,10},{10,1... | collective-permute-start | bytes 460808 | tf_op jit(solution)/shard_map/ppermute | solution.py:14
  38.2 11.6 %collective-permute-start.3 = (f32[10,10,384]{2,1,0:T(8,128)S(1)}, f32[10,10,384]{2,1,0:T(8,128)S(1)}, u32[]{:S(2)}, u32[]{:S(2)}) collective-permute-start(f32[10,10,384]{2,1,0:T(8,128)S(1)} %get-tuple-element.167), channel_id=1, source_target_pairs={{1,0},{2,1},{3,2},{4,3},{5,4},{6,5},{7,6},{8,7},{9,8},{10,9},{11,1... | collective-permute-start | bytes 460808 | tf_op jit(solution)/shard_map/ppermute | solution.py:17
  89.8 0.8 copy-start.1
  89.8 0.8 copy-start.2
  89.8 0.8 copy-start.3
  89.8 0.8 copy-start.4
  89.9 0.8 copy-start.5
  89.9 0.8 copy-start.6
  89.9 0.8 copy-start.7
  89.9 0.8 copy-start.8
  89.9 0.8 copy-start.9
  92.7 0.7 copy-start.10
  92.7 0.7 copy-start.11
  92.7 0.7 copy-start.12
  92.7 0.7 copy-start.13
  92.7 0.7 copy-start.14
  92.7 0.8 copy-start.15
  95.9 1.8 %copy-start.22 = (s32[1024]{0:T(1024)S(1)}, s32[1024]{0:T(1024)}, u32[]{:S(2)}) copy-start(s32[1024]{0:T(1024)} %get-tuple-element.189) | copy-start | bytes 12292
  105.7 4.1 %copy-start.24 = (pred[15,64]{1,0:T(8,128)(4,1)S(1)}, pred[15,64]{1,0:T(8,128)(4,1)}, u32[]{:S(2)}) copy-start(pred[15,64]{1,0:T(8,128)(4,1)} %get-tuple-element.185) | copy-start | bytes 2884
  109.8 4.3 %copy-start.19 = (f32[10,10]{1,0:T(8,128)S(1)}, f32[10,10]{1,0:T(8,128)}, u32[]{:S(2)}) copy-start(f32[10,10]{1,0:T(8,128)} %fusion.11) | copy-start | bytes 1204
  114.0 1.1 copy-start.18
  114.1 1.1 copy-start.17
  114.4 12.3 %copy-start.21 = (s32[1024]{0:T(1024)S(1)}, s32[1024]{0:T(1024)}, u32[]{:S(2)}) copy-start(s32[1024]{0:T(1024)} %copy-done.20) | copy-start | bytes 12292
  114.5 13.4 %copy-start.26 = (pred[448]{0:T(512)(128)(4,1)S(1)}, pred[448]{0:T(512)(128)(4,1)}, u32[]{:S(2)}) copy-start(pred[448]{0:T(512)(128)(4,1)} %copy-done.25) | copy-start | bytes 1348
  115.2 10.9 %collective-permute-start.6 = (f32[10,64]{1,0:T(8,128)S(1)}, f32[10,64]{1,0:T(8,128)S(1)}, u32[]{:S(2)}, u32[]{:S(2)}) collective-permute-start(f32[10,64]{1,0:T(8,128)S(1)} %add.210), channel_id=1, source_target_pairs={{0,1},{1,2},{2,3},{3,4},{4,5},{5,6},{6,7},{7,8},{8,9},{9,10},{10,1... | collective-permute-start | bytes 7688 | tf_op jit(solution)/shard_map/ppermute | solution.py:14
  117.1 9.4 %collective-permute-start.7 = (f32[10,64]{1,0:T(8,128)S(1)}, f32[10,64]{1,0:T(8,128)S(1)}, u32[]{:S(2)}, u32[]{:S(2)}) collective-permute-start(f32[10,64]{1,0:T(8,128)S(1)} %add.210), channel_id=1, source_target_pairs={{1,0},{2,1},{3,2},{4,3},{5,4},{6,5},{7,6},{8,7},{9,8},{10,9},{11,1... | collective-permute-start | bytes 7688 | tf_op jit(solution)/shard_map/ppermute | solution.py:17
where the time goes:
time: 130 us; the launch traced here: 129 us
  local copies, waits for them, and re-layouts  64.4 us (50%)
  starting transfers between devices  41.5 us (32%)
  other arithmetic  18.8 us (14%)
  waiting for transfers between devices  2.41 us (2%)
  between operations  1.79 us (1%)
    ppermute x4, starting transfers between devices, with_halo(): lax.ppermute(lax.slice_in_dim(block, 0, width, axis=dim), axis, backward)  33.7 us
    transpose x10, local copies, waits for them, and re-layouts, block_product(): jnp.swapaxes(right[inner], 0, 1)[:, None, :, :]  21.1 us
    gather x7, local copies, waits for them, and re-layouts, gather_cells(): taken = jnp.take(flat, index.reshape(-1), axis=1)  19.6 us
    slice x1, local copies, waits for them, and re-layouts, block_product(): right[inner]  7.99 us
    ppermute x4, starting transfers between devices, with_halo(): lax.ppermute(lax.slice_in_dim(block, block.shape[dim] - width, None, axis...  7.8 us
    reduce_sum x1, other arithmetic, body(): coarse_op = jnp.sum(gathered * weight, axis=3)  4.19 us
    add x2, local copies, waits for them, and re-layouts, body(): per_slot = term if per_slot is None else per_slot + term  3.17 us
    add x1, other arithmetic, block_product(): total = term if total is None else total + term  3.01 us
  transfers between devices with their start and end apart: 8, of which 3 were waited for; matrix products, arithmetic and copies ran while one was open for 13% of the time, Pallas kernels for 0%

commit v1 on v0

v1 whole, which is shorter than its diff:
```python
import functools

import jax
import jax.numpy as jnp
from jax import lax
from jax.experimental import pallas as pl
from jax.experimental.pallas import tpu as pltpu
from jax.sharding import PartitionSpec as P

F32 = jnp.float32
BF16 = jnp.bfloat16
MESH = pl.DeviceIdType.MESH
LANES = 128


def lane_gather(table, index):
    return jnp.take_along_axis(table, index, axis=1, mode="promise_in_bounds")


def halves(value):
    high = value.astype(BF16)
    low = (value - high.astype(F32)).astype(BF16)
    return high, low


def dot_nn(left, right):
    return lax.dot_general(left, right, (((1,), (0,)), ((), ())), preferred_element_type=F32)


def dot_nt(left, right):
    return lax.dot_general(left, right, (((1,), (1,)), ((), ())), preferred_element_type=F32)


def kernel(
    n_fine, n_coarse,
    a_hbm, col_hbm, slot_hbm, ghost_hbm, p_hbm, mem_hbm, cc_hbm, rhs_hbm, guess_hbm,
    op_ref, it_ref,
    a_v, col_v, slot_v, ghost_v, p_v, mem_v, cc_v, rhs_v, guess_v,
    v_pad, rhs_pad, v_one, v_near, v_far,
    mt_s, m_s, w_own, w_near, w_far, pc_own, pc_near, pc_far,
    q_s, d_s, inv_s, idx_s, cc_s, oh_own, oh_near, oh_far,
    phl_s, whl_s, wacc_s, wg_s, acc_s, g_s, prod_s, z_s, lhs_s, rt_s, op_s,
    in_sem, send_sem, recv_sem,
):
    n_all = n_fine * n_coarse
    me = lax.axis_index("fine") * n_coarse + lax.axis_index("coarse")
    odd = lax.rem(me, 2)
    near = me + 1 - 2 * odd
    far = lax.rem(me + n_all - 1 + 2 * odd, n_all)
    near_id = (near // n_coarse, lax.rem(near, n_coarse))
    far_id = (far // n_coarse, lax.rem(far, n_coarse))

    barrier = pltpu.get_barrier_semaphore()
    pl.semaphore_signal(barrier, inc=1, device_id=far_id, device_id_type=MESH)
    pl.semaphore_signal(barrier, inc=1, device_id=near_id, device_id_type=MESH)

    order, agg_count = rhs_v.shape
    fine_rows = a_v.shape[2]
    slots = cc_v.shape[0]
    cells = p_v.shape[2]
    tiles = cells // LANES
    rows = pc_own.shape[0]
    span = rows * 8
    rest = fine_rows - 1

    pairs = [(p_hbm, p_v), (mem_hbm, mem_v), (guess_hbm, guess_v), (col_hbm, col_v), (ghost_hbm, ghost_v),
             (slot_hbm, slot_v), (cc_hbm, cc_v), (rhs_hbm, rhs_v), (a_hbm, a_v)]
    loads = [pltpu.make_async_copy(src, dst, in_sem.at[i]) for i, (src, dst) in enumerate(pairs)]
    for load in loads:
        load.start()

    loads[1].wait()
    cell_row = lax.broadcasted_iota(jnp.int32, (cells, agg_count), 0)
    found = None
    for place in range(mem_v.shape[0]):
        hit = cell_row == mem_v[place:place + 1, :]
        found = hit if found is None else jnp.logical_or(found, hit)
    mt_s[...] = jnp.where(found, 1.0, 0.0).astype(BF16)
    eye = jnp.where(
        lax.broadcasted_iota(jnp.int32, (agg_count, agg_count), 0)
        == lax.broadcasted_iota(jnp.int32, (agg_count, agg_count), 1), 1.0, 0.0).astype(BF16)
    m_s[...] = dot_nt(eye, mt_s[...]).astype(BF16)

    loads[2].wait()
    v_pad[...] = jnp.zeros_like(v_pad)
    v_pad[0:order, :] = guess_v[...]
    high, low = halves(v_pad[...])
    v_cells = (dot_nn(high, m_s[...]) + dot_nn(low, m_s[...]))[0:order, :]
    loads[0].wait()
    w_own[...] = jnp.zeros_like(w_own)
    for j in range(order):
        w_own[j:j + 1, :] = jnp.sum(p_v[j] * v_cells, axis=0, keepdims=True)
    pc_own[...] = jnp.zeros_like(pc_own)
    for j in range(order):
        pc_own[order * j:order * (j + 1), :] = p_v[j]

    pl.semaphore_wait(barrier, 2)

    def send(source, to_near, to_far, base):
        made = []
        for at, (dst, ident) in enumerate(((to_far, far_id), (to_near, near_id))):
            copy = pltpu.make_async_remote_copy(
                src_ref=source, dst_ref=dst, send_sem=send_sem.at[base + at], recv_sem=recv_sem.at[base + at],
                device_id=ident, device_id_type=MESH)
            copy.start()
            made.append(copy)
        return made

    w_sent = send(w_own, w_near, w_far, 0)
    p_sent = send(pc_own, pc_near, pc_far, 2)

    loads[8].wait()

    def q_step(step, carry):
        pair = step // tiles
        lanes = pl.ds(pl.multiple_of(lax.rem(step, tiles) * LANES, LANES), LANES)
        blocks = [[a_v[r, pair * 2 + jj, :, lanes] for r in range(order)] for jj in range(2)]
        for i in range(order):
            total = [None, None]
            for r in range(order):
                basis = p_v[r, i:i + 1, lanes]
                for jj in range(2):
                    term = basis * blocks[jj][r]
                    total[jj] = term if total[jj] is None else total[jj] + term
            for jj in range(2):
                q_s[i, pair * 2 + jj, :, lanes] = total[jj]
        return carry

    lax.fori_loop(0, order // 2 * tiles, q_step, 0)

    d_s[...] = jnp.zeros_like(d_s)

    def d_step(i, carry):
        total = None
        for j in range(order):
            term = q_s[i, j, 0:1, :] * p_v[j]
            total = term if total is None else total + term
        d_s[i, 0:order, :] = total
        return carry

    lax.fori_loop(0, order, d_step, 0)
    deep = d_s.shape[1]
    high, low = halves(d_s[...].reshape(order * deep, cells))
    diagonal = (dot_nt(high, m_s[...]) + dot_nt(low, m_s[...])).reshape(order, deep, agg_count)
    wide = jnp.zeros((order, LANES - agg_count), F32)
    for i in range(order):
        op_s[pl.ds(i * order * 8, order, stride=8), :] = jnp.concatenate([diagonal[i, 0:order, :], wide], axis=1)
    inverse = diagonal
    entry = lax.broadcasted_iota(jnp.int32, (deep, agg_count), 0)
    row_at = lax.broadcasted_iota(jnp.int32, (order, 1, agg_count), 0)
    for pivot in range(order):
        line = inverse[pivot]
        scale = 1.0 / line[pivot:pivot + 1, :]
        line = jnp.where(entry == pivot, 1.0, line) * scale
        factor = inverse[:, pivot:pivot + 1, :]
        kept = jnp.where((entry == pivot)[None], 0.0, inverse)
        inverse = kept - factor * line[None]
        inverse = jnp.where(row_at == pivot, line[None], inverse)
    inv_s[...] = inverse

    loads[3].wait()
    loads[4].wait()
    idx_s[...] = jnp.zeros_like(idx_s)
    idx_s[0, 0:fine_rows, :] = col_v[...]
    is_odd = jnp.full((8, LANES), odd, jnp.int32)
    half = ghost_v.shape[0] * LANES // 2
    for t in range(tiles):
        at = slice(t * LANES, (t + 1) * LANES)
        col = idx_s[0, :, at]
        place = jnp.maximum(col - cells, 0)
        lane = jnp.bitwise_and(place, LANES - 1)
        part = jnp.right_shift(place, 7)
        cell = jnp.zeros((8, LANES), jnp.int32)
        for b in range(ghost_v.shape[0]):
            got = lane_gather(jnp.broadcast_to(ghost_v[b:b + 1, :], (8, LANES)), lane)
            cell = jnp.where(part == b, got, cell)
        own = col < cells
        after = jnp.where(col >= cells + half, 1, 0)
        same = after != is_odd
        idx_s[1, :, at] = jnp.where(own, col, -1)
        idx_s[2, :, at] = jnp.where(jnp.logical_and(jnp.logical_not(own), same), cell, -1)
        idx_s[3, :, at] = jnp.where(jnp.logical_or(own, same), -1, cell)
    ramp = lax.broadcasted_iota(jnp.int32, (256, cells), 0).astype(F32).astype(BF16)
    one = jnp.ones((256, cells), BF16)
    zero = jnp.zeros((256, cells), BF16)
    for group, hot in ((1, oh_own), (2, oh_near), (3, oh_far)):
        for k in range(rest):
            for block in range(cells // 256):
                line = (idx_s[group, k + 1:k + 2, :] - 256 * block).astype(F32).astype(BF16)
                hot[256 * block:256 * (block + 1), k * cells:(k + 1) * cells] = jnp.where(ramp == line, one, zero)

    loads[5].wait()
    member = m_s[...]
    none = jnp.zeros_like(member)
    for k in range(rest):
        line = slot_v[k + 1:k + 2, :].astype(F32).astype(BF16)
        wide_line = jnp.broadcast_to(line, (agg_count, cells))
        for s in range(1, slots):
            picked = wide_line == jnp.full((agg_count, cells), s, BF16)
            rt_s[(s - 1) * agg_count:s * agg_count, k * cells:(k + 1) * cells] = jnp.where(picked, member, none)

    def split_basis(source):
        high, low = halves(source[...])
        phl_s[0:rows, :] = high
        phl_s[rows:2 * rows, :] = low

    def basis_part(hot, k):
        both = dot_nn(phl_s[...], hot[:, k * cells:(k + 1) * cells])
        return both[0:rows, :] + both[rows:2 * rows, :]

    def vector_part(source, hot, k):
        both = dot_nn(whl_s[...], hot[:, k * cells:(k + 1) * cells])
        return both[0:16, :] + both[16:32, :]

    def split_vector(source):
        high, low = halves(source[...])
        whl_s[0:16, :] = high
        whl_s[16:32, :] = low

    split_basis(pc_own)
    split_vector(w_own)
    for k in range(rest):
        at = slice(k * cells, (k + 1) * cells)
        acc_s[:, at] = basis_part(oh_own, k)
        wacc_s[:, at] = vector_part(w_own, oh_own, k)
    w_sent[1].wait_recv()
    split_vector(w_near)
    for k in range(rest):
        at = slice(k * cells, (k + 1) * cells)
        wacc_s[:, at] += vector_part(w_near, oh_near, k)
    p_sent[1].wait_recv()
    split_basis(pc_near)
    for k in range(rest):
        at = slice(k * cells, (k + 1) * cells)
        acc_s[:, at] += basis_part(oh_near, k)

    loads[7].wait()
    rhs_pad[...] = jnp.zeros_like(rhs_pad)
    rhs_pad[0:order, :] = rhs_v[...]
    z_s[...] = jnp.zeros_like(z_s)
    for t in range(tiles):
        wg_s[pl.ds(t * LANES, 16, stride=8), :] = w_own[:, t * LANES:(t + 1) * LANES]
    w_sent[0].wait_recv()
    split_vector(w_far)
    for k in range(rest):
        total = wacc_s[:, k * cells:(k + 1) * cells] + vector_part(w_far, oh_far, k)
        for t in range(tiles):
            wg_s[pl.ds(t * LANES + k + 1, 16, stride=8), :] = total[:, t * LANES:(t + 1) * LANES]
    for t in range(tiles):
        at = slice(t * LANES, (t + 1) * LANES)
        taken = [wg_s[t * LANES + j * 8:t * LANES + j * 8 + fine_rows, :] for j in range(order)]
        for i in range(order):
            total = None
            for j in range(order):
                term = q_s[i, j, :, at] * taken[j]
                total = term if total is None else total + term
            z_s[i:i + 1, at] = jnp.sum(total, axis=0, keepdims=True)
    high, low = halves(z_s[...])
    applied = dot_nt(high, m_s[...]) + dot_nt(low, m_s[...])
    residual = rhs_pad[...] - applied
    v_one[...] = jnp.zeros_like(v_one)
    for i in range(order):
        update = jnp.sum(inv_s[i] * residual, axis=0, keepdims=True)
        v_one[i:i + 1, 0:agg_count] = v_pad[i:i + 1, :] + update
    v_sent = send(v_one, v_near, v_far, 4)

    p_sent[0].wait_recv()
    split_basis(pc_far)
    for k in range(rest):
        total = acc_s[:, k * cells:(k + 1) * cells] + basis_part(oh_far, k)
        for t in range(tiles):
            g_s[pl.ds(t * span + k + 1, rows, stride=8), :] = total[:, t * LANES:(t + 1) * LANES]

    def product_step(step, carry):
        pair = step // tiles
        t = lax.rem(step, tiles)
        lanes = pl.ds(pl.multiple_of(t * LANES, LANES), LANES)
        base = t * span + pair * 16
        taken = [[g_s[pl.ds(pl.multiple_of(base + (j * order + ll) * 8, 8), fine_rows), :] for j in range(order)]
                 for ll in range(2)]
        for i in range(order):
            total = [None, None]
            for j in range(order):
                left = q_s[i, j, :, lanes]
                for ll in range(2):
                    term = left * taken[ll][j]
                    total[ll] = term if total[ll] is None else total[ll] + term
            for ll in range(2):
                prod_s[pl.ds(pl.multiple_of(base + (i * order + ll) * 8, 8), fine_rows), :] = total[ll]
        return carry

    lax.fori_loop(0, order // 2 * tiles, product_step, 0)
    for k in range(rest):
        for t in range(tiles):
            high, low = halves(prod_s[pl.ds(t * span + k + 1, rows, stride=8), :])
            at = slice(k * cells + t * LANES, k * cells + (t + 1) * LANES)
            lhs_s[0:rows, at] = high
            lhs_s[rows:2 * rows, at] = low
    both = dot_nt(lhs_s[...], rt_s[...])
    summed = both[0:rows, :] + both[rows:2 * rows, :]
    filler = jnp.zeros((order * order, LANES - agg_count), F32)
    for s in range(1, slots):
        part = summed[0:order * order, (s - 1) * agg_count:s * agg_count]
        op_s[pl.ds(s, order * order, stride=8), :] = jnp.concatenate([part, filler], axis=1)
    for i in range(order):
        for l in range(order):
            op_ref[i, l] = op_s[(i * order + l) * 8:(i * order + l) * 8 + slots, 0:agg_count]

    loads[6].wait()
    cc_s[...] = jnp.zeros_like(cc_s)
    cc_s[0:slots, 0:agg_count] = cc_v[...]
    column = cc_s[...]
    lane = jnp.bitwise_and(column, agg_count - 1)
    holder = column // agg_count
    is_near = holder == 2 - 2 * is_odd
    is_far = holder == 2 * is_odd
    first = lane + jnp.where(is_near, agg_count, 0)
    v_sent[1].wait_recv()
    v_sent[0].wait_recv()
    nearby = jnp.concatenate([v_one[:, 0:agg_count], v_near[:, 0:agg_count]], axis=1)
    distant = v_far[...]
    names = []
    for l in range(order):
        one_side = lane_gather(jnp.broadcast_to(nearby[l:l + 1, :], (8, LANES)), first)
        other = lane_gather(jnp.broadcast_to(distant[l:l + 1, :], (8, LANES)), lane)
        names.append(jnp.where(is_far, other, one_side)[0:slots, 0:agg_count])
    lines = []
    z2 = rhs_pad
    for i in range(order):
        total = None
        for l in range(order):
            term = op_s[(i * order + l) * 8:(i * order + l) * 8 + slots, 0:agg_count] * names[l]
            total = term if total is None else total + term
        z2[i:i + 1, :] = rhs_v[i:i + 1, :] - jnp.sum(total, axis=0, keepdims=True)
    residual = z2[...]
    for i in range(order):
        update = jnp.sum(inv_s[i] * residual, axis=0, keepdims=True)
        it_ref[i:i + 1, :] = v_one[i:i + 1, 0:agg_count] + update
    for copy in w_sent + p_sent + v_sent:
        copy.wait_send()


def body(n_fine, n_coarse, fine_blocks, fine_columns, coarse_slots, ghost_lists, tentative, members, coarse_columns,
         coarse_rhs, coarse_guess):
    fine_rows, order, _, cells = fine_blocks.shape
    slots, agg_count = coarse_columns.shape
    rest = fine_rows - 1
    ghosts = ghost_lists.reshape(-1, LANES)
    rows = -(-order * order // 16) * 16
    vm = pltpu.VMEM
    scratch = [
        vm((order, order, fine_rows, cells), F32), vm(fine_columns.shape, jnp.int32), vm(coarse_slots.shape, jnp.int32),
        vm(ghosts.shape, jnp.int32), vm(tentative.shape, F32), vm(members.shape, jnp.int32),
        vm(coarse_columns.shape, jnp.int32), vm(coarse_rhs.shape, F32), vm(coarse_guess.shape, F32),
        vm((16, agg_count), F32), vm((16, agg_count), F32),
        vm((16, LANES), F32), vm((16, LANES), F32), vm((16, LANES), F32),
        vm((cells, agg_count), BF16), vm((agg_count, cells), BF16),
        vm((16, cells), F32), vm((16, cells), F32), vm((16, cells), F32),
        vm((rows, cells), F32), vm((rows, cells), F32), vm((rows, cells), F32),
        vm((order, order, fine_rows, cells), F32), vm((order, 16, cells), F32), vm((order, 16, agg_count), F32),
        vm((4, 8, cells), jnp.int32), vm((8, LANES), jnp.int32),
        vm((cells, rest * cells), BF16), vm((cells, rest * cells), BF16), vm((cells, rest * cells), BF16),
        vm((2 * rows, cells), BF16), vm((32, cells), BF16), vm((16, rest * cells), F32),
        vm((cells // LANES * LANES, LANES), F32),
        vm((rows, rest * cells), F32),
        vm((cells // LANES * rows * 8, LANES), F32), vm((cells // LANES * rows * 8, LANES), F32),
        vm((16, cells), F32), vm((2 * rows, rest * cells), BF16), vm((rest * agg_count, rest * cells), BF16),
        vm((order * order * 8, LANES), F32),
        pltpu.SemaphoreType.DMA((9,)), pltpu.SemaphoreType.DMA((6,)), pltpu.SemaphoreType.DMA((6,)),
    ]
    op, iterate = pl.pallas_call(
        functools.partial(kernel, n_fine, n_coarse),
        out_shape=(jax.ShapeDtypeStruct((order, order, slots, agg_count), F32),
                   jax.ShapeDtypeStruct((order, agg_count), F32)),
        in_specs=[pl.BlockSpec(memory_space=pl.ANY)] * 9,
        out_specs=[pl.BlockSpec(memory_space=pltpu.VMEM)] * 2,
        scratch_shapes=scratch,
        compiler_params=pltpu.CompilerParams(collective_id=0, has_side_effects=True, vmem_limit_bytes=56 * 2**20),
    )(jnp.transpose(fine_blocks, (1, 2, 0, 3)), fine_columns, coarse_slots, ghosts, tentative, members, coarse_columns,
      coarse_rhs, coarse_guess)
    return jnp.transpose(op, (2, 0, 1, 3)), iterate


def solution(mesh):
    both = ("fine", "coarse")
    placed = (
        P(None, None, None, both), P(None, both), P(None, both), P(both), P(None, None, both), P(None, both),
        P(None, both), P(None, both), P(None, both),
    )
    return jax.shard_map(
        functools.partial(body, mesh.shape["fine"], mesh.shape["coarse"]),
        mesh=mesh,
        in_specs=placed,
        out_specs=(P(None, None, None, both), P(None, both)),
        check_vma=False,
    )
```

time: 130 us -> 24.5 us (0.19)
  the two profiles are of different devices: /device:TPU:6 before, /device:TPU:0 now
where the time goes in v1:
time: 24.5 us; the launch traced here: 24.3 us
  Pallas kernels  20.6 us (84%)
  local copies, waits for them, and re-layouts  3.08 us (13%)
  between operations  0.64 us (3%)
    pallas_call x1, Pallas kernels, body(): pl.pallas_call(functools.partial(kernel, n_fine, n_coarse), out_shape=(ja...  20.6 us
    unnamed x2, local copies, waits for them, and re-layouts  3.08 us

profile of v1, /device:TPU:0, one launch (start us, length us, event | category | flops | bytes accessed | tf_op | source)
XLA Modules:
  0.0 24.3 jit_solution(9239842618569336536)
XLA Ops:
  0.6 20.6 %shard_map.104 = (f32[10,10,7,64]{3,2,1,0:T(8,128)}, f32[10,64]{1,0:T(8,128)}) custom-call(f32[10,10,7,512]{3,2,1,0:T(8,128)} %bitcast.3, s32[7,512]{1,0:T(8,128)} %col_hbm.1, s32[7,512]{1,0:T(8,128)} %slot_hbm.1, s32[6,128]{1,0:T(8,128)} %bitcast.5, f32[10,10,512]{2,1,0:T(8,128)} %p_hbm.1, s32[15,64]{1,0:T(8,128)} %mem_hbm.1, s32[7,64]{1,0:T(8,128)} %cc_hbm.1, ...), custom_call_target="tpu_custom_call" | custom-call | tf_op jit(solution)/shard_map/pallas_call | solution.py:371
  21.3 1.8 %copy.13 = f32[7,10,10,64]{3,0,2,1:T(8,128)} copy(f32[7,10,10,64]{3,0,2,1:T(8,128)} %bitcast.4) | data formatting | bytes 358400
  23.0 1.3 %copy.14 = f32[10,64]{1,0:T(8,128)} copy(f32[10,64]{1,0:T(8,128)} %get-tuple-element.9) | data formatting | bytes 5120

commit v2 on v1

--- a/solution.py
+++ b/solution.py
@@ -33,13 +33,13 @@
 
 def kernel(
     n_fine, n_coarse,
-    a_hbm, col_hbm, slot_hbm, ghost_hbm, p_hbm, mem_hbm, cc_hbm, rhs_hbm, guess_hbm,
-    op_ref, it_ref,
-    a_v, col_v, slot_v, ghost_v, p_v, mem_v, cc_v, rhs_v, guess_v,
-    v_pad, rhs_pad, v_one, v_near, v_far,
+    a_hbm, col_hbm, slot_hbm, ghost_hbm, p_hbm, mem_hbm, rhs_hbm, guess_hbm,
+    op_s, small_s,
+    a_v, col_v, slot_v, ghost_v, p_v, mem_v, rhs_v, guess_v,
+    v_pad, v_one, v_near, v_far,
     mt_s, m_s, w_own, w_near, w_far, pc_own, pc_near, pc_far,
-    q_s, d_s, inv_s, idx_s, cc_s, oh_own, oh_near, oh_far,
-    phl_s, whl_s, wacc_s, wg_s, acc_s, g_s, prod_s, z_s, lhs_s, rt_s, op_s,
+    q_s, d_s, idx_s, oh_own, oh_near, oh_far,
+    phl_s, whl_s, wacc_s, wg_s, acc_s, g_s, prod_s, z_s, lhs_s, rt_s,
     in_sem, send_sem, recv_sem,
 ):
     n_all = n_fine * n_coarse
@@ -50,13 +50,20 @@
     near_id = (near // n_coarse, lax.rem(near, n_coarse))
     far_id = (far // n_coarse, lax.rem(far, n_coarse))
 
+    has_far = jnp.logical_and(jnp.logical_or(odd == 1, me > 0), jnp.logical_or(odd == 0, me < n_all - 1))
+    early = lax.rem(me, 8 * n_coarse) == 0
+
     barrier = pltpu.get_barrier_semaphore()
-    pl.semaphore_signal(barrier, inc=1, device_id=far_id, device_id_type=MESH)
+
+    @pl.when(has_far)
+    def greet():
+        pl.semaphore_signal(barrier, inc=1, device_id=far_id, device_id_type=MESH)
+
     pl.semaphore_signal(barrier, inc=1, device_id=near_id, device_id_type=MESH)
 
     order, agg_count = rhs_v.shape
+    slots = 1 + rt_s.shape[0] // agg_count
     fine_rows = a_v.shape[2]
-    slots = cc_v.shape[0]
     cells = p_v.shape[2]
     tiles = cells // LANES
     rows = pc_own.shape[0]
@@ -64,7 +71,8 @@
     rest = fine_rows - 1
 
     pairs = [(p_hbm, p_v), (mem_hbm, mem_v), (guess_hbm, guess_v), (col_hbm, col_v), (ghost_hbm, ghost_v),
-             (slot_hbm, slot_v), (cc_hbm, cc_v), (rhs_hbm, rhs_v), (a_hbm, a_v)]
+             (slot_hbm, slot_v), (rhs_hbm, rhs_v)]
+    pairs += [(a_hbm.at[:, 2 * b:2 * b + 2], a_v.at[:, 2 * b:2 * b + 2]) for b in range(order // 2)]
     loads = [pltpu.make_async_copy(src, dst, in_sem.at[i]) for i, (src, dst) in enumerate(pairs)]
     for load in loads:
         load.start()
@@ -94,25 +102,48 @@
     for j in range(order):
         pc_own[order * j:order * (j + 1), :] = p_v[j]
 
-    pl.semaphore_wait(barrier, 2)
-
-    def send(source, to_near, to_far, base):
-        made = []
-        for at, (dst, ident) in enumerate(((to_far, far_id), (to_near, near_id))):
-            copy = pltpu.make_async_remote_copy(
-                src_ref=source, dst_ref=dst, send_sem=send_sem.at[base + at], recv_sem=recv_sem.at[base + at],
-                device_id=ident, device_id_type=MESH)
-            copy.start()
-            made.append(copy)
-        return made
-
-    w_sent = send(w_own, w_near, w_far, 0)
-    p_sent = send(pc_own, pc_near, pc_far, 2)
-
-    loads[8].wait()
+    def exchange(source, to_near, to_far, base):
+        return [pltpu.make_async_remote_copy(
+            src_ref=source, dst_ref=dst, send_sem=send_sem.at[base + at], recv_sem=recv_sem.at[base + at],
+            device_id=ident, device_id_type=MESH)
+            for at, (dst, ident) in enumerate(((to_far, far_id), (to_near, near_id)))]
+
+    def launch(copies):
+        @pl.when(has_far)
+        def start_far():
+            copies[0].start()
+
+        copies[1].start()
+
+    def await_far(copy, landing):
+        @pl.when(has_far)
+        def take():
+            copy.wait_recv()
+
+        @pl.when(jnp.logical_not(has_far))
+        def clear():
+            landing[...] = jnp.zeros_like(landing)
+
+    w_sent = exchange(w_own, w_near, w_far, 0)
+    p_sent = exchange(pc_own, pc_near, pc_far, 2)
+    v_sent = exchange(v_one, v_near, v_far, 4)
+
+    def handshake():
+        pl.semaphore_wait(barrier, 1 + has_far.astype(jnp.int32))
+        launch(w_sent)
+        launch(p_sent)
+
+    @pl.when(jnp.logical_not(early))
+    def greet_now():
+        handshake()
 
     def q_step(step, carry):
         pair = step // tiles
+
+        @pl.when(lax.rem(step, tiles) == 0)
+        def arrive():
+            pltpu.make_async_copy(a_hbm.at[:, pl.ds(pair * 2, 2)], a_v.at[:, pl.ds(pair * 2, 2)], in_sem.at[7 + pair]).wait()
+
         lanes = pl.ds(pl.multiple_of(lax.rem(step, tiles) * LANES, LANES), LANES)
         blocks = [[a_v[r, pair * 2 + jj, :, lanes] for r in range(order)] for jj in range(2)]
         for i in range(order):
@@ -145,8 +176,8 @@
     wide = jnp.zeros((order, LANES - agg_count), F32)
     for i in range(order):
         op_s[pl.ds(i * order * 8, order, stride=8), :] = jnp.concatenate([diagonal[i, 0:order, :], wide], axis=1)
-    inverse = diagonal
-    entry = lax.broadcasted_iota(jnp.int32, (deep, agg_count), 0)
+    inverse = jnp.stack([op_s[pl.ds(l * 8, order, stride=order * 8), :][:, 0:agg_count] for l in range(order)])
+    entry = lax.broadcasted_iota(jnp.int32, (order, agg_count), 0)
     row_at = lax.broadcasted_iota(jnp.int32, (order, 1, agg_count), 0)
     for pivot in range(order):
         line = inverse[pivot]
@@ -156,7 +187,8 @@
         kept = jnp.where((entry == pivot)[None], 0.0, inverse)
         inverse = kept - factor * line[None]
         inverse = jnp.where(row_at == pivot, line[None], inverse)
-    inv_s[...] = inverse
+    for i in range(order):
+        small_s[16 * i + 32:16 * i + 32 + order, 0:agg_count] = inverse[i]
 
     loads[3].wait()
     loads[4].wait()
@@ -217,35 +249,35 @@
         whl_s[0:16, :] = high
         whl_s[16:32, :] = low
 
-    split_basis(pc_own)
     split_vector(w_own)
     for k in range(rest):
-        at = slice(k * cells, (k + 1) * cells)
-        acc_s[:, at] = basis_part(oh_own, k)
-        wacc_s[:, at] = vector_part(w_own, oh_own, k)
+        wacc_s[:, k * cells:(k + 1) * cells] = vector_part(w_own, oh_own, k)
+
+    def own_basis():
+        split_basis(pc_own)
+        for k in range(rest):
+            acc_s[:, k * cells:(k + 1) * cells] = basis_part(oh_own, k)
+
+    @pl.when(early)
+    def greet_late():
+        own_basis()
+        handshake()
+
     w_sent[1].wait_recv()
     split_vector(w_near)
     for k in range(rest):
-        at = slice(k * cells, (k + 1) * cells)
-        wacc_s[:, at] += vector_part(w_near, oh_near, k)
-    p_sent[1].wait_recv()
-    split_basis(pc_near)
-    for k in range(rest):
-        at = slice(k * cells, (k + 1) * cells)
-        acc_s[:, at] += basis_part(oh_near, k)
-
-    loads[7].wait()
-    rhs_pad[...] = jnp.zeros_like(rhs_pad)
-    rhs_pad[0:order, :] = rhs_v[...]
-    z_s[...] = jnp.zeros_like(z_s)
+        wacc_s[:, k * cells:(k + 1) * cells] += vector_part(w_near, oh_near, k)
     for t in range(tiles):
         wg_s[pl.ds(t * LANES, 16, stride=8), :] = w_own[:, t * LANES:(t + 1) * LANES]
-    w_sent[0].wait_recv()
+    loads[6].wait()
+    await_far(w_sent[0], w_far)
+
     split_vector(w_far)
     for k in range(rest):
         total = wacc_s[:, k * cells:(k + 1) * cells] + vector_part(w_far, oh_far, k)
         for t in range(tiles):
             wg_s[pl.ds(t * LANES + k + 1, 16, stride=8), :] = total[:, t * LANES:(t + 1) * LANES]
+
     for t in range(tiles):
         at = slice(t * LANES, (t + 1) * LANES)
         taken = [wg_s[t * LANES + j * 8:t * LANES + j * 8 + fine_rows, :] for j in range(order)]
@@ -254,17 +286,28 @@
             for j in range(order):
                 term = q_s[i, j, :, at] * taken[j]
                 total = term if total is None else total + term
-            z_s[i:i + 1, at] = jnp.sum(total, axis=0, keepdims=True)
+            z_s[8 * i:8 * i + fine_rows, at] = total
+
     high, low = halves(z_s[...])
     applied = dot_nt(high, m_s[...]) + dot_nt(low, m_s[...])
-    residual = rhs_pad[...] - applied
+    update = v_pad[0:order, :]
+    for j in range(order):
+        line = rhs_v[j:j + 1, :] - jnp.sum(applied[8 * j:8 * j + fine_rows], axis=0, keepdims=True)
+        update = update + small_s[16 * j + 32:16 * j + 32 + order, 0:agg_count] * line
     v_one[...] = jnp.zeros_like(v_one)
-    for i in range(order):
-        update = jnp.sum(inv_s[i] * residual, axis=0, keepdims=True)
-        v_one[i:i + 1, 0:agg_count] = v_pad[i:i + 1, :] + update
-    v_sent = send(v_one, v_near, v_far, 4)
-
-    p_sent[0].wait_recv()
+    v_one[0:order, 0:agg_count] = update
+    launch(v_sent)
+
+    @pl.when(jnp.logical_not(early))
+    def own_late():
+        own_basis()
+
+    p_sent[1].wait_recv()
+    split_basis(pc_near)
+    for k in range(rest):
+        acc_s[:, k * cells:(k + 1) * cells] += basis_part(oh_near, k)
+    await_far(p_sent[0], pc_far)
+
     split_basis(pc_far)
     for k in range(rest):
         total = acc_s[:, k * cells:(k + 1) * cells] + basis_part(oh_far, k)
@@ -302,11 +345,24 @@
     for s in range(1, slots):
         part = summed[0:order * order, (s - 1) * agg_count:s * agg_count]
         op_s[pl.ds(s, order * order, stride=8), :] = jnp.concatenate([part, filler], axis=1)
-    for i in range(order):
-        for l in range(order):
-            op_ref[i, l] = op_s[(i * order + l) * 8:(i * order + l) * 8 + slots, 0:agg_count]
-
-    loads[6].wait()
+
+    v_sent[1].wait_recv()
+    small_s[0:16, :] = jnp.concatenate([v_one[:, 0:agg_count], v_near[:, 0:agg_count]], axis=1)
+    await_far(v_sent[0], v_far)
+    small_s[16:32, :] = v_far[...]
+    for copies in (w_sent, p_sent, v_sent):
+        copies[1].wait_send()
+
+        @pl.when(has_far)
+        def drain():
+            copies[0].wait_send()
+
+
+def finish(n_fine, n_coarse, op_s, small_s, cc_v, rhs_v, op_ref, it_ref, cc_s):
+    odd = lax.rem(lax.axis_index("coarse"), 2)
+    is_odd = jnp.full((8, LANES), odd, jnp.int32)
+    order, agg_count = rhs_v.shape
+    slots = cc_v.shape[0]
     cc_s[...] = jnp.zeros_like(cc_s)
     cc_s[0:slots, 0:agg_count] = cc_v[...]
     column = cc_s[...]
@@ -315,29 +371,22 @@
     is_near = holder == 2 - 2 * is_odd
     is_far = holder == 2 * is_odd
     first = lane + jnp.where(is_near, agg_count, 0)
-    v_sent[1].wait_recv()
-    v_sent[0].wait_recv()
-    nearby = jnp.concatenate([v_one[:, 0:agg_count], v_near[:, 0:agg_count]], axis=1)
-    distant = v_far[...]
     names = []
     for l in range(order):
-        one_side = lane_gather(jnp.broadcast_to(nearby[l:l + 1, :], (8, LANES)), first)
-        other = lane_gather(jnp.broadcast_to(distant[l:l + 1, :], (8, LANES)), lane)
+        one_side = lane_gather(jnp.broadcast_to(small_s[l:l + 1, :], (8, LANES)), first)
+        other = lane_gather(jnp.broadcast_to(small_s[16 + l:17 + l, :], (8, LANES)), lane)
         names.append(jnp.where(is_far, other, one_side)[0:slots, 0:agg_count])
-    lines = []
-    z2 = rhs_pad
+    update = small_s[0:order, 0:agg_count]
     for i in range(order):
         total = None
         for l in range(order):
-            term = op_s[(i * order + l) * 8:(i * order + l) * 8 + slots, 0:agg_count] * names[l]
+            block = op_s[(i * order + l) * 8:(i * order + l) * 8 + slots, 0:agg_count]
+            op_ref[i, l] = block
+            term = block * names[l]
             total = term if total is None else total + term
-        z2[i:i + 1, :] = rhs_v[i:i + 1, :] - jnp.sum(total, axis=0, keepdims=True)
-    residual = z2[...]
-    for i in range(order):
-        update = jnp.sum(inv_s[i] * residual, axis=0, keepdims=True)
-        it_ref[i:i + 1, :] = v_one[i:i + 1, 0:agg_count] + update
-    for copy in w_sent + p_sent + v_sent:
-        copy.wait_send()
+        line = rhs_v[i:i + 1, :] - jnp.sum(total, axis=0, keepdims=True)
+        update = update + small_s[16 * i + 32:16 * i + 32 + order, 0:agg_count] * line
+    it_ref[...] = update
 
 
 def body(n_fine, n_coarse, fine_blocks, fine_columns, coarse_slots, ghost_lists, tentative, members, coarse_columns,
@@ -351,33 +400,42 @@
     scratch = [
         vm((order, order, fine_rows, cells), F32), vm(fine_columns.shape, jnp.int32), vm(coarse_slots.shape, jnp.int32),
         vm(ghosts.shape, jnp.int32), vm(tentative.shape, F32), vm(members.shape, jnp.int32),
-        vm(coarse_columns.shape, jnp.int32), vm(coarse_rhs.shape, F32), vm(coarse_guess.shape, F32),
-        vm((16, agg_count), F32), vm((16, agg_count), F32),
+        vm(coarse_rhs.shape, F32), vm(coarse_guess.shape, F32),
+        vm((16, agg_count), F32),
         vm((16, LANES), F32), vm((16, LANES), F32), vm((16, LANES), F32),
         vm((cells, agg_count), BF16), vm((agg_count, cells), BF16),
         vm((16, cells), F32), vm((16, cells), F32), vm((16, cells), F32),
         vm((rows, cells), F32), vm((rows, cells), F32), vm((rows, cells), F32),
-        vm((order, order, fine_rows, cells), F32), vm((order, 16, cells), F32), vm((order, 16, agg_count), F32),
-        vm((4, 8, cells), jnp.int32), vm((8, LANES), jnp.int32),
+        vm((order, order, fine_rows, cells), F32), vm((order, 16, cells), F32),
+        vm((4, 8, cells), jnp.int32),
         vm((cells, rest * cells), BF16), vm((cells, rest * cells), BF16), vm((cells, rest * cells), BF16),
         vm((2 * rows, cells), BF16), vm((32, cells), BF16), vm((16, rest * cells), F32),
         vm((cells // LANES * LANES, LANES), F32),
         vm((rows, rest * cells), F32),
         vm((cells // LANES * rows * 8, LANES), F32), vm((cells // LANES * rows * 8, LANES), F32),
-        vm((16, cells), F32), vm((2 * rows, rest * cells), BF16), vm((rest * agg_count, rest * cells), BF16),
-        vm((order * order * 8, LANES), F32),
-        pltpu.SemaphoreType.DMA((9,)), pltpu.SemaphoreType.DMA((6,)), pltpu.SemaphoreType.DMA((6,)),
+        vm((8 * order, cells), F32), vm((2 * rows, rest * cells), BF16), vm(((slots - 1) * agg_count, rest * cells), BF16),
+        pltpu.SemaphoreType.DMA((7 + order // 2,)), pltpu.SemaphoreType.DMA((6,)), pltpu.SemaphoreType.DMA((6,)),
     ]
+    in_vmem = pl.BlockSpec(memory_space=pltpu.VMEM)
+    padded, small = pl.pallas_call(
+        functools.partial(kernel, n_fine, n_coarse),
+        out_shape=(vm((order * order * 8, LANES), F32), vm((16 * order + 32, LANES), F32)),
+        in_specs=[pl.BlockSpec(memory_space=pltpu.HBM)] * 8,
+        out_specs=[in_vmem] * 2,
+        scratch_shapes=scratch,
+        compiler_params=pltpu.CompilerParams(collective_id=0, has_side_effects=True, vmem_limit_bytes=40 * 2**20),
+    )(*[pltpu.with_memory_space_constraint(given, pltpu.HBM) for given in (
+        jnp.transpose(fine_blocks, (1, 2, 0, 3)), fine_columns, coarse_slots, ghosts, tentative, members, coarse_rhs,
+        coarse_guess)])
     op, iterate = pl.pallas_call(
-        functools.partial(kernel, n_fine, n_coarse),
+        functools.partial(finish, n_fine, n_coarse),
         out_shape=(jax.ShapeDtypeStruct((order, order, slots, agg_count), F32),
                    jax.ShapeDtypeStruct((order, agg_count), F32)),
-        in_specs=[pl.BlockSpec(memory_space=pl.ANY)] * 9,
-        out_specs=[pl.BlockSpec(memory_space=pltpu.VMEM)] * 2,
-        scratch_shapes=scratch,
-        compiler_params=pltpu.CompilerParams(collective_id=0, has_side_effects=True, vmem_limit_bytes=56 * 2**20),
-    )(jnp.transpose(fine_blocks, (1, 2, 0, 3)), fine_columns, coarse_slots, ghosts, tentative, members, coarse_columns,
-      coarse_rhs, coarse_guess)
+        in_specs=[in_vmem] * 4,
+        out_specs=[in_vmem] * 2,
+        scratch_shapes=[vm((8, LANES), jnp.int32)],
+        compiler_params=pltpu.CompilerParams(vmem_limit_bytes=8 * 2**20),
+    )(padded, small, coarse_columns, coarse_rhs)
     return jnp.transpose(op, (2, 0, 1, 3)), iterate
 
 

time: 24.5 us -> 19.9 us (0.81)
  the two profiles are of different devices: /device:TPU:0 before, /device:TPU:6 now
where the time goes in v2:
time: 19.9 us; the launch traced here: 19.8 us
  Pallas kernels  19.1 us (96%)
  between operations  0.67 us (3%)
    pallas_call x1, Pallas kernels, body(): pl.pallas_call(functools.partial(kernel, n_fine, n_coarse), out_shape=(vm...  18.3 us
    pallas_call x1, Pallas kernels, body(): pl.pallas_call(functools.partial(finish, n_fine, n_coarse), out_shape=(ja...  0.82 us

profile of v2, /device:TPU:6, one launch (start us, length us, event | category | flops | bytes accessed | tf_op | source)
XLA Modules:
  0.0 19.8 jit_solution(1499115125298529983)
XLA Ops:
  0.6 0.0 copy-start
  0.6 0.0 copy-start.1
  0.7 18.3 %shard_map.104 = (f32[800,128]{1,0:T(8,128)S(1)}, f32[192,128]{1,0:T(8,128)S(1)}) custom-call(f32[10,10,7,512]{3,2,1,0:T(8,128)} %bitcast.3, s32[7,512]{1,0:T(8,128)} %col_hbm.1, s32[7,512]{1,0:T(8,128)} %slot_hbm.1, s32[6,128]{1,0:T(8,128)} %bitcast.4, f32[10,10,512]{2,1,0:T(8,128)} %p_hbm.1, s32[15,64]{1,0:T(8,128)} %mem_hbm.1, f32[10,64]{1,0:T(8,128)} %rhs_v.1, ...), custom_call_target="tpu_custom_call" | custom-call | tf_op jit(solution)/shard_map/pallas_call | solution.py:420
  18.9 0.0 copy-done
  18.9 0.0 copy-done.1
  18.9 0.8 %shard_map.105 = (f32[10,10,7,64]{3,2,1,0:T(8,128)}, f32[10,64]{1,0:T(8,128)}) custom-call(f32[800,128]{1,0:T(8,128)S(1)} %get-tuple-element.6.op_s, f32[192,128]{1,0:T(8,128)S(1)} %get-tuple-element.7.small_s, s32[7,64]{1,0:T(8,128)S(1)} %copy-done.1, f32[10,64]{1,0:T(8,128)S(1)} %copy-done), custom_call_target="tpu_custom_call" | custom-call | tf_op jit(solution)/shard_map/pallas_call | solution.py:430
Async XLA Ops:
  0.6 18.3 %copy-start = (f32[10,64]{1,0:T(8,128)S(1)}, f32[10,64]{1,0:T(8,128)}, u32[]{:S(2)}) copy-start(f32[10,64]{1,0:T(8,128)} %rhs_v.1) | copy-start | bytes 7684
  0.6 18.3 %copy-start.1 = (s32[7,64]{1,0:T(8,128)S(1)}, s32[7,64]{1,0:T(8,128)}, u32[]{:S(2)}) copy-start(s32[7,64]{1,0:T(8,128)} %cc_v.1) | copy-start | bytes 5380

commit v3 on v2

v3 whole, which is shorter than its diff:
```python
import functools

import jax
import jax.numpy as jnp
from jax import lax
from jax.experimental import pallas as pl
from jax.experimental.pallas import tpu as pltpu
from jax.sharding import PartitionSpec as P

F32 = jnp.float32
BF16 = jnp.bfloat16
MESH = pl.DeviceIdType.MESH
LANES = 128


def lane_gather(table, index):
    return jnp.take_along_axis(table, index, axis=1, mode="promise_in_bounds")


def column_parts(order):
    return (0,), (order,)


def halves(value):
    high = value.astype(BF16)
    low = (value - high.astype(F32)).astype(BF16)
    return high, low


def dot_nn(left, right):
    return lax.dot_general(left, right, (((1,), (0,)), ((), ())), preferred_element_type=F32)


def dot_nt(left, right):
    return lax.dot_general(left, right, (((1,), (1,)), ((), ())), preferred_element_type=F32)


def kernel(
    n_fine, n_coarse,
    a_hbm, col_hbm, slot_hbm, ghost_hbm, p_hbm, mem_hbm, rhs_hbm, guess_hbm,
    op_s, small_s,
    a_v, col_v, slot_v, ghost_v, p_v, mem_v, rhs_v, guess_v,
    v_pad, v_one, v_near, v_far,
    mt_s, m_s, w_own, w_near, w_far, w_held, pc_own, pc_near, pc_far,
    q_s, ap_s, d_s, idx_s, oh_own, oh_near, oh_far,
    phl_s, whl_s, wacc_s, wg_s, acc_s, g_s, prod_s, z_s, lhs_s, rt_s,
    in_sem, send_sem, recv_sem, met_sem,
):
    n_all = n_fine * n_coarse
    me = lax.axis_index("fine") * n_coarse + lax.axis_index("coarse")
    odd = lax.rem(me, 2)
    near = me + 1 - 2 * odd
    far = lax.rem(me + n_all - 1 + 2 * odd, n_all)
    near_id = (near // n_coarse, lax.rem(near, n_coarse))
    far_id = (far // n_coarse, lax.rem(far, n_coarse))

    has_far = jnp.logical_and(jnp.logical_or(odd == 1, me > 0), jnp.logical_or(odd == 0, me < n_all - 1))
    lap = 8 * n_coarse
    heads = jnp.logical_and(lax.rem(me, lap) == 0, me > 0)
    tails = jnp.logical_and(lax.rem(me, lap) == lap - 1, me < n_all - 1)
    bridges = jnp.logical_and(lax.rem(me, lap) == n_coarse - 1, me < n_all - lap)
    lap_head = lax.rem((me // lap + 1) * lap, n_all)
    head_id = (lap_head // n_coarse, lax.rem(lap_head, n_coarse))
    lap_tail = (me // lap + 1) * lap - 1
    tail_id = (lap_tail // n_coarse, lax.rem(lap_tail, n_coarse))
    bridge = jnp.where(heads, me - lap, me // lap * lap) + n_coarse - 1
    bridge_id = (bridge // n_coarse, lax.rem(bridge, n_coarse))
    lazy = me == 1

    barrier = pltpu.get_barrier_semaphore()

    @pl.when(jnp.logical_and(has_far, jnp.logical_not(tails)))
    def greet():
        pl.semaphore_signal(barrier, inc=1, device_id=far_id, device_id_type=MESH)

    pl.semaphore_signal(barrier, inc=1, device_id=near_id, device_id_type=MESH)

    @pl.when(bridges)
    def greet_lap():
        pl.semaphore_signal(barrier, inc=1, device_id=tail_id, device_id_type=MESH)
        pl.semaphore_signal(barrier, inc=1, device_id=head_id, device_id_type=MESH)

    order, agg_count = rhs_v.shape
    slots = 1 + rt_s.shape[0] // agg_count
    fine_rows = a_v.shape[2]
    cells = p_v.shape[2]
    tiles = cells // LANES
    firsts, counts = column_parts(order)
    sent = [-(-count * order // 8) * 8 for count in counts]
    tall = [-(-count * order // 16) * 16 for count in counts]
    at_row = (0,)
    op_row = (0,)
    parts = len(counts)
    span = prod_s.shape[0] // tiles
    rest = fine_rows - 1

    pairs = [(p_hbm, p_v), (mem_hbm, mem_v), (guess_hbm, guess_v), (col_hbm, col_v), (ghost_hbm, ghost_v),
             (slot_hbm, slot_v), (rhs_hbm, rhs_v)]
    pairs += [(a_hbm.at[:, 2 * b:2 * b + 2], a_v.at[:, 2 * b:2 * b + 2]) for b in range(order // 2)]
    loads = [pltpu.make_async_copy(src, dst, in_sem.at[i]) for i, (src, dst) in enumerate(pairs)]
    for load in loads:
        load.start()

    def exchange(source, to_near, to_far, base):
        return [pltpu.make_async_remote_copy(
            src_ref=source, dst_ref=dst, send_sem=send_sem.at[base + at], recv_sem=recv_sem.at[base + at],
            device_id=ident, device_id_type=MESH)
            for at, (dst, ident) in enumerate(((to_far, far_id), (to_near, near_id)))]

    def launch_far(copies):
        @pl.when(has_far)
        def start_far():
            copies[0].start()

    def await_far(copy, landing):
        @pl.when(has_far)
        def take():
            copy.wait_recv()

        @pl.when(jnp.logical_not(has_far))
        def clear():
            landing[...] = jnp.zeros_like(landing)

    w_sent = exchange(w_own, w_near, w_far, 0)
    v_sent = exchange(v_one, v_near, v_far, 2)
    p_sent = [exchange(*(ref.at[at_row[c]:at_row[c] + sent[c]] for ref in (pc_own, pc_near, pc_far)), 4 + 2 * c)
              for c in range(parts)]
    w_up = pltpu.make_async_remote_copy(
        src_ref=w_own, dst_ref=w_held, send_sem=send_sem.at[8], recv_sem=recv_sem.at[8],
        device_id=bridge_id, device_id_type=MESH)
    w_over = pltpu.make_async_remote_copy(
        src_ref=w_held, dst_ref=w_far, send_sem=send_sem.at[9], recv_sem=recv_sem.at[0],
        device_id=tail_id, device_id_type=MESH)

    def await_barrier():
        pl.semaphore_wait(barrier, 1 + has_far.astype(jnp.int32) + tails.astype(jnp.int32))

    def send_basis():
        for copies in p_sent:
            @pl.when(jnp.logical_not(heads))
            def start_now():
                launch_far(copies)

            copies[1].start()

    def send_vector():
        @pl.when(jnp.logical_not(heads))
        def start_direct():
            launch_far(w_sent)

        @pl.when(heads)
        def start_up():
            w_up.start()

        w_sent[1].start()

    loads[0].wait()
    pc_own[...] = jnp.zeros_like(pc_own)
    for c in range(parts):
        for j in range(order):
            spot = at_row[c] + counts[c] * j
            pc_own[spot:spot + counts[c], :] = p_v[j, firsts[c]:firsts[c] + counts[c], :]

    @pl.when(jnp.logical_not(lazy))
    def meet():
        await_barrier()

        @pl.when(tails)
        def announce():
            pl.semaphore_signal(met_sem, inc=1, device_id=bridge_id, device_id_type=MESH)
            pl.semaphore_signal(met_sem, inc=1, device_id=far_id, device_id_type=MESH)

    loads[1].wait()
    cell_row = lax.broadcasted_iota(jnp.int32, (cells, agg_count), 0)
    found = None
    for place in range(mem_v.shape[0]):
        hit = cell_row == mem_v[place:place + 1, :]
        found = hit if found is None else jnp.logical_or(found, hit)
    mt_s[...] = jnp.where(found, 1.0, 0.0).astype(BF16)
    eye = jnp.where(
        lax.broadcasted_iota(jnp.int32, (agg_count, agg_count), 0)
        == lax.broadcasted_iota(jnp.int32, (agg_count, agg_count), 1), 1.0, 0.0).astype(BF16)
    m_s[...] = dot_nt(eye, mt_s[...]).astype(BF16)

    loads[2].wait()
    v_pad[...] = jnp.zeros_like(v_pad)
    v_pad[0:order, :] = guess_v[...]
    high, low = halves(v_pad[...])
    v_cells = (dot_nn(high, m_s[...]) + dot_nn(low, m_s[...]))[0:order, :]
    w_own[...] = jnp.zeros_like(w_own)
    for j in range(order):
        w_own[j:j + 1, :] = jnp.sum(p_v[j] * v_cells, axis=0, keepdims=True)

    @pl.when(jnp.logical_not(lazy))
    def tell():
        send_vector()
        send_basis()

    loads[3].wait()
    loads[4].wait()
    idx_s[...] = jnp.zeros_like(idx_s)
    idx_s[0, 0:fine_rows, :] = col_v[...]
    is_odd = jnp.full((8, LANES), odd, jnp.int32)
    half = ghost_v.shape[0] * LANES // 2
    for t in range(tiles):
        at = slice(t * LANES, (t + 1) * LANES)
        col = idx_s[0, :, at]
        place = jnp.maximum(col - cells, 0)
        lane = jnp.bitwise_and(place, LANES - 1)
        part = jnp.right_shift(place, 7)
        cell = jnp.zeros((8, LANES), jnp.int32)
        for b in range(ghost_v.shape[0]):
            got = lane_gather(jnp.broadcast_to(ghost_v[b:b + 1, :], (8, LANES)), lane)
            cell = jnp.where(part == b, got, cell)
        own = col < cells
        after = jnp.where(col >= cells + half, 1, 0)
        same = after != is_odd
        idx_s[1, :, at] = jnp.where(own, col, -1)
        idx_s[2, :, at] = jnp.where(jnp.logical_and(jnp.logical_not(own), same), cell, -1)
        idx_s[3, :, at] = jnp.where(jnp.logical_or(own, same), -1, cell)
    ramp = lax.broadcasted_iota(jnp.int32, (256, cells), 0).astype(F32).astype(BF16)
    one = jnp.ones((256, cells), BF16)
    zero = jnp.zeros((256, cells), BF16)
    for group, hot in ((1, oh_own), (2, oh_near), (3, oh_far)):
        for k in range(rest):
            for block in range(cells // 256):
                line = (idx_s[group, k + 1:k + 2, :] - 256 * block).astype(F32).astype(BF16)
                hot[256 * block:256 * (block + 1), k * cells:(k + 1) * cells] = jnp.where(ramp == line, one, zero)

    def split_basis(source, c):
        high, low = halves(source[at_row[c]:at_row[c] + tall[c], :])
        phl_s[0:tall[c], 0:cells] = high
        phl_s[0:tall[c], cells:2 * cells] = low

    def basis_part(hot, c, k):
        hot_part = hot[:, k * cells:(k + 1) * cells]
        return dot_nn(phl_s[0:tall[c], :], jnp.concatenate([hot_part, hot_part], axis=0))

    def vector_part(hot, k):
        both = dot_nn(whl_s[...], hot[:, k * cells:(k + 1) * cells])
        return both[0:16, :] + both[16:32, :]

    def split_vector(source):
        high, low = halves(source[...])
        whl_s[0:16, :] = high
        whl_s[16:32, :] = low

    split_vector(w_own)
    for k in range(rest):
        wacc_s[:, k * cells:(k + 1) * cells] = vector_part(oh_own, k)
    for t in range(tiles):
        wg_s[pl.ds(t * LANES, 16, stride=8), :] = w_own[:, t * LANES:(t + 1) * LANES]

    for b in range(order // 2):
        loads[7 + b].wait()
    d_s[...] = jnp.zeros_like(d_s)
    for t in range(tiles):
        at = slice(t * LANES, (t + 1) * LANES)
        for r in range(order):
            total = None
            for j in range(order):
                term = a_v[r, j, 0:1, at] * p_v[j, :, at]
                total = term if total is None else total + term
            ap_s[r, 0:order, :] = total
        for i in range(order):
            total = None
            for r in range(order):
                term = p_v[r, i:i + 1, at] * ap_s[r, 0:order, :]
                total = term if total is None else total + term
            d_s[i, 0:order, at] = total
    deep = d_s.shape[1]
    high, low = halves(d_s[...].reshape(order * deep, cells))
    diagonal = (dot_nt(high, m_s[...]) + dot_nt(low, m_s[...])).reshape(order, deep, agg_count)
    wide = jnp.zeros((order, LANES - agg_count), F32)
    for i in range(order):
        for c in range(parts):
            line = jnp.concatenate([diagonal[i, firsts[c]:firsts[c] + counts[c], :], wide[0:counts[c]]], axis=1)
            op_s[pl.ds((op_row[c] + i * counts[c]) * 8, counts[c], stride=8), :] = line
    inverse = jnp.stack([op_s[pl.ds((op_row[c] + l) * 8, order, stride=counts[c] * 8), :][:, 0:agg_count]
                         for c in range(parts) for l in range(counts[c])])
    entry = lax.broadcasted_iota(jnp.int32, (order, agg_count), 0)
    row_at = lax.broadcasted_iota(jnp.int32, (order, 1, agg_count), 0)
    for pivot in range(order):
        line = inverse[pivot]
        scale = 1.0 / line[pivot:pivot + 1, :]
        line = jnp.where(entry == pivot, 1.0, line) * scale
        factor = inverse[:, pivot:pivot + 1, :]
        kept = jnp.where((entry == pivot)[None], 0.0, inverse)
        inverse = kept - factor * line[None]
        inverse = jnp.where(row_at == pivot, line[None], inverse)
    for i in range(order):
        small_s[16 * i + 32:16 * i + 32 + order, 0:agg_count] = inverse[i]

    loads[6].wait()
    z_s[...] = jnp.zeros_like(z_s)
    v_one[...] = jnp.zeros_like(v_one)

    def sweep():
        w_sent[1].wait_recv()
        split_vector(w_near)
        for k in range(rest):
            wacc_s[:, k * cells:(k + 1) * cells] += vector_part(oh_near, k)

        await_far(w_sent[0], w_far)
        split_vector(w_far)
        for k in range(rest):
            total = wacc_s[:, k * cells:(k + 1) * cells] + vector_part(oh_far, k)
            for t in range(tiles):
                wg_s[pl.ds(t * LANES + k + 1, 16, stride=8), :] = total[:, t * LANES:(t + 1) * LANES]

        for t in range(tiles):
            at = slice(t * LANES, (t + 1) * LANES)
            taken = [wg_s[t * LANES + j * 8:t * LANES + j * 8 + fine_rows, :] for j in range(order)]
            whole = None
            for r in range(order):
                total = None
                for j in range(order):
                    term = a_v[r, j, :, at] * taken[j]
                    total = term if total is None else total + term
                term = p_v[r, :, at] * jnp.sum(total, axis=0, keepdims=True)
                whole = term if whole is None else whole + term
            z_s[0:order, at] = whole

        high, low = halves(z_s[...])
        whl_s[0:16, :] = high
        whl_s[16:32, :] = low
        both = dot_nt(whl_s[...], m_s[...])
        residual = rhs_v[...] - (both[0:order, :] + both[16:16 + order, :])
        update = v_pad[0:order, :]
        for j in range(order):
            update = update + small_s[16 * j + 32:16 * j + 32 + order, 0:agg_count] * residual[j:j + 1, :]
        v_one[0:order, 0:agg_count] = update
        launch_far(v_sent)
        v_sent[1].start()

    def prepare():
        loads[5].wait()
        member = m_s[...]
        none = jnp.zeros_like(member)
        for k in range(rest):
            line = slot_v[k + 1:k + 2, :].astype(F32).astype(BF16)
            wide_line = jnp.broadcast_to(line, (agg_count, cells))
            for s in range(1, slots):
                picked = wide_line == jnp.full((agg_count, cells), s, BF16)
                rt_s[(s - 1) * agg_count:s * agg_count, k * cells:(k + 1) * cells] = jnp.where(picked, member, none)

        def q_step(step, carry):
            pair = step // tiles

            lanes = pl.ds(pl.multiple_of(lax.rem(step, tiles) * LANES, LANES), LANES)
            blocks = [[a_v[r, pair * 2 + jj, :, lanes] for r in range(order)] for jj in range(2)]
            for i in range(order):
                total = [None, None]
                for r in range(order):
                    basis = p_v[r, i:i + 1, lanes]
                    for jj in range(2):
                        term = basis * blocks[jj][r]
                        total[jj] = term if total[jj] is None else total[jj] + term
                for jj in range(2):
                    q_s[i, pair * 2 + jj, :, lanes] = total[jj]
            return carry

        lax.fori_loop(0, order // 2 * tiles, q_step, 0)

        @pl.when(lazy)
        def meet_late():
            await_barrier()
            send_vector()
            send_basis()

        @pl.when(bridges)
        def hand_on():
            w_up.wait_recv()
            pl.semaphore_wait(met_sem, 1)
            w_over.start()

        for c in range(parts):
            split_basis(pc_own, c)
            for k in range(rest):
                acc_s[at_row[c]:at_row[c] + tall[c], k * cells:(k + 1) * cells] = basis_part(oh_own, c, k)
        for c in range(parts):
            p_sent[c][1].wait_recv()
            split_basis(pc_near, c)
            for k in range(rest):
                acc_s[at_row[c]:at_row[c] + tall[c], k * cells:(k + 1) * cells] += basis_part(oh_near, c, k)

        @pl.when(heads)
        def start_late():
            pl.semaphore_wait(met_sem, 1)
            for copies in p_sent:
                copies[0].start()

    def turn(at, carry):
        @pl.when(jnp.logical_xor(at == 0, tails))
        def run_prepare():
            prepare()

        @pl.when(at == 0)
        def run_sweep():
            sweep()

        return carry

    lax.fori_loop(0, 2, turn, 0)

    def product_part(c):
        pairs_here = counts[c] // 2

        def product_step(step, carry):
            pair = step // tiles
            t = lax.rem(step, tiles)
            lanes = pl.ds(pl.multiple_of(t * LANES, LANES), LANES)
            base = t * span + pair * 16
            taken = [[g_s[pl.ds(pl.multiple_of(base + (j * counts[c] + ll) * 8, 8), fine_rows), :]
                      for j in range(order)] for ll in range(2)]
            for i in range(order):
                total = [None, None]
                for j in range(order):
                    left = q_s[i, j, :, lanes]
                    for ll in range(2):
                        term = left * taken[ll][j]
                        total[ll] = term if total[ll] is None else total[ll] + term
                for ll in range(2):
                    prod_s[pl.ds(pl.multiple_of(base + (i * counts[c] + ll) * 8, 8), fine_rows), :] = total[ll]
            return carry

        lax.fori_loop(0, pairs_here * tiles, product_step, 0)

    for c in range(parts):
        await_far(p_sent[c][0], pc_far.at[at_row[c]:at_row[c] + tall[c]])
        split_basis(pc_far, c)
        height = counts[c] * order
        for k in range(rest):
            total = acc_s[at_row[c]:at_row[c] + tall[c], k * cells:(k + 1) * cells] + basis_part(oh_far, c, k)
            for t in range(tiles):
                g_s[pl.ds(t * span + k + 1, height, stride=8), :] = total[0:height, t * LANES:(t + 1) * LANES]
        product_part(c)
        for k in range(rest):
            for t in range(tiles):
                high, low = halves(prod_s[pl.ds(t * span + k + 1, tall[c], stride=8), :])
                at = slice(k * cells + t * LANES, k * cells + (t + 1) * LANES)
                lhs_s[0:tall[c], at] = high
                lhs_s[tall[c]:2 * tall[c], at] = low
        both = dot_nt(lhs_s[0:2 * tall[c], :], rt_s[...])
        summed = both[0:height, :] + both[tall[c]:tall[c] + height, :]
        filler = jnp.zeros((height, LANES - agg_count), F32)
        for s in range(1, slots):
            part = summed[:, (s - 1) * agg_count:s * agg_count]
            op_s[pl.ds(op_row[c] * 8 + s, height, stride=8), :] = jnp.concatenate([part, filler], axis=1)

    v_sent[1].wait_recv()
    small_s[0:16, :] = jnp.concatenate([v_one[:, 0:agg_count], v_near[:, 0:agg_count]], axis=1)
    await_far(v_sent[0], v_far)
    small_s[16:32, :] = v_far[...]
    for copies in [v_sent] + p_sent:
        copies[1].wait_send()

        @pl.when(has_far)
        def drain():
            copies[0].wait_send()

    w_sent[1].wait_send()

    @pl.when(jnp.logical_and(has_far, jnp.logical_not(heads)))
    def drain_direct():
        w_sent[0].wait_send()

    @pl.when(heads)
    def drain_up():
        w_up.wait_send()

    @pl.when(bridges)
    def drain_over():
        w_over.wait_send()


def finish(n_fine, n_coarse, op_s, small_s, cc_v, rhs_v, op_ref, it_ref, cc_s):
    odd = lax.rem(lax.axis_index("coarse"), 2)
    is_odd = jnp.full((8, LANES), odd, jnp.int32)
    order, agg_count = rhs_v.shape
    slots = cc_v.shape[0]
    cc_s[...] = jnp.zeros_like(cc_s)
    cc_s[0:slots, 0:agg_count] = cc_v[...]
    column = cc_s[...]
    lane = jnp.bitwise_and(column, agg_count - 1)
    holder = column // agg_count
    is_near = holder == 2 - 2 * is_odd
    is_far = holder == 2 * is_odd
    first = lane + jnp.where(is_near, agg_count, 0)
    names = []
    for l in range(order):
        one_side = lane_gather(jnp.broadcast_to(small_s[l:l + 1, :], (8, LANES)), first)
        other = lane_gather(jnp.broadcast_to(small_s[16 + l:17 + l, :], (8, LANES)), lane)
        names.append(jnp.where(is_far, other, one_side)[0:slots, 0:agg_count])
    update = small_s[0:order, 0:agg_count]
    for i in range(order):
        total = None
        for l in range(order):
            row = (i * order + l) * 8
            block = op_s[row:row + slots, 0:agg_count]
            op_ref[i, l] = block
            term = block * names[l]
            total = term if total is None else total + term
        line = rhs_v[i:i + 1, :] - jnp.sum(total, axis=0, keepdims=True)
        update = update + small_s[16 * i + 32:16 * i + 32 + order, 0:agg_count] * line
    it_ref[...] = update


def body(n_fine, n_coarse, fine_blocks, fine_columns, coarse_slots, ghost_lists, tentative, members, coarse_columns,
         coarse_rhs, coarse_guess):
    fine_rows, order, _, cells = fine_blocks.shape
    slots, agg_count = coarse_columns.shape
    rest = fine_rows - 1
    ghosts = ghost_lists.reshape(-1, LANES)
    deep = -(-order * order // 16) * 16
    vm = pltpu.VMEM
    scratch = [
        vm((order, order, fine_rows, cells), F32), vm(fine_columns.shape, jnp.int32), vm(coarse_slots.shape, jnp.int32),
        vm(ghosts.shape, jnp.int32), vm(tentative.shape, F32), vm(members.shape, jnp.int32),
        vm(coarse_rhs.shape, F32), vm(coarse_guess.shape, F32),
        vm((16, agg_count), F32),
        vm((16, LANES), F32), vm((16, LANES), F32), vm((16, LANES), F32),
        vm((cells, agg_count), BF16), vm((agg_count, cells), BF16),
        vm((16, cells), F32), vm((16, cells), F32), vm((16, cells), F32), vm((16, cells), F32),
        vm((deep, cells), F32), vm((deep, cells), F32), vm((deep, cells), F32),
        vm((order, order, fine_rows, cells), F32), vm((order, 16, LANES), F32), vm((order, 16, cells), F32),
        vm((4, 8, cells), jnp.int32),
        vm((cells, rest * cells), BF16), vm((cells, rest * cells), BF16), vm((cells, rest * cells), BF16),
        vm((deep, 2 * cells), BF16), vm((32, cells), BF16), vm((16, rest * cells), F32),
        vm((cells // LANES * LANES, LANES), F32),
        vm((deep, rest * cells), F32),
        vm((cells // LANES * deep * 8, LANES), F32), vm((cells // LANES * deep * 8, LANES), F32),
        vm((16, cells), F32), vm((2 * deep, rest * cells), BF16), vm(((slots - 1) * agg_count, rest * cells), BF16),
        pltpu.SemaphoreType.DMA((7 + order // 2,)), pltpu.SemaphoreType.DMA((10,)), pltpu.SemaphoreType.DMA((9,)),
        pltpu.SemaphoreType.REGULAR,
    ]
    in_vmem = pl.BlockSpec(memory_space=pltpu.VMEM)
    padded, small = pl.pallas_call(
        functools.partial(kernel, n_fine, n_coarse),
        out_shape=(vm((order * order * 8, LANES), F32), vm((16 * order + 32, LANES), F32)),
        in_specs=[pl.BlockSpec(memory_space=pltpu.HBM)] * 8,
        out_specs=[in_vmem] * 2,
        scratch_shapes=scratch,
        compiler_params=pltpu.CompilerParams(collective_id=0, has_side_effects=True, vmem_limit_bytes=40 * 2**20),
    )(*[pltpu.with_memory_space_constraint(given, pltpu.HBM) for given in (
        jnp.transpose(fine_blocks, (1, 2, 0, 3)), fine_columns, coarse_slots, ghosts, tentative, members, coarse_rhs,
        coarse_guess)])
    op, iterate = pl.pallas_call(
        functools.partial(finish, n_fine, n_coarse),
        out_shape=(jax.ShapeDtypeStruct((order, order, slots, agg_count), F32),
                   jax.ShapeDtypeStruct((order, agg_count), F32)),
        in_specs=[in_vmem] * 4,
        out_specs=[in_vmem] * 2,
        scratch_shapes=[vm((8, LANES), jnp.int32)],
        compiler_params=pltpu.CompilerParams(vmem_limit_bytes=8 * 2**20),
    )(padded, small, coarse_columns, coarse_rhs)
    return jnp.transpose(op, (2, 0, 1, 3)), iterate


def solution(mesh):
    both = ("fine", "coarse")
    placed = (
        P(None, None, None, both), P(None, both), P(None, both), P(both), P(None, None, both), P(None, both),
        P(None, both), P(None, both), P(None, both),
    )
    return jax.shard_map(
        functools.partial(body, mesh.shape["fine"], mesh.shape["coarse"]),
        mesh=mesh,
        in_specs=placed,
        out_specs=(P(None, None, None, both), P(None, both)),
        check_vma=False,
    )
```

time: 19.9 us -> 19.6 us (0.985)
  Pallas kernels: 19.1 us -> 18.8 us
    pallas_call x1, Pallas kernels: 18.3 us -> 18 us  [body(): pl.pallas_call(functools.partial(kernel, n_fine, n_coarse), out_shape=(vm...]
where the time goes in v3:
time: 19.6 us; the launch traced here: 19.5 us
  Pallas kernels  18.8 us (96%)
  between operations  0.67 us (3%)
    pallas_call x1, Pallas kernels, body(): pl.pallas_call(functools.partial(kernel, n_fine, n_coarse), out_shape=(vm...  18 us
    pallas_call x1, Pallas kernels, body(): pl.pallas_call(functools.partial(finish, n_fine, n_coarse), out_shape=(ja...  0.82 us

profile of v3, /device:TPU:6, one launch (start us, length us, event | category | flops | bytes accessed | tf_op | source)
XLA Modules:
  0.0 19.5 jit_solution(14596351336484643303)
XLA Ops:
  0.6 0.0 copy-start
  0.6 0.0 copy-start.1
  0.7 18.0 %shard_map.104 = (f32[800,128]{1,0:T(8,128)S(1)}, f32[192,128]{1,0:T(8,128)S(1)}) custom-call(f32[10,10,7,512]{3,2,1,0:T(8,128)} %bitcast.3, s32[7,512]{1,0:T(8,128)} %col_hbm.1, s32[7,512]{1,0:T(8,128)} %slot_hbm.1, s32[6,128]{1,0:T(8,128)} %bitcast.4, f32[10,10,512]{2,1,0:T(8,128)} %p_hbm.1, s32[15,64]{1,0:T(8,128)} %mem_hbm.1, f32[10,64]{1,0:T(8,128)} %rhs_v.1, ...), custom_call_target="tpu_custom_call" | custom-call | tf_op jit(solution)/shard_map/pallas_call | solution.py:538
  18.7 0.0 copy-done
  18.7 0.0 copy-done.1
  18.7 0.8 %shard_map.105 = (f32[10,10,7,64]{3,2,1,0:T(8,128)}, f32[10,64]{1,0:T(8,128)}) custom-call(f32[800,128]{1,0:T(8,128)S(1)} %get-tuple-element.6.op_s, f32[192,128]{1,0:T(8,128)S(1)} %get-tuple-element.7.small_s, s32[7,64]{1,0:T(8,128)S(1)} %copy-done.1, f32[10,64]{1,0:T(8,128)S(1)} %copy-done), custom_call_target="tpu_custom_call" | custom-call | tf_op jit(solution)/shard_map/pallas_call | solution.py:548
Async XLA Ops:
  0.6 18.0 %copy-start = (f32[10,64]{1,0:T(8,128)S(1)}, f32[10,64]{1,0:T(8,128)}, u32[]{:S(2)}) copy-start(f32[10,64]{1,0:T(8,128)} %rhs_v.1) | copy-start | bytes 7684
  0.6 18.0 %copy-start.1 = (s32[7,64]{1,0:T(8,128)S(1)}, s32[7,64]{1,0:T(8,128)}, u32[]{:S(2)}) copy-start(s32[7,64]{1,0:T(8,128)} %cc_v.1) | copy-start | bytes 5380

commit v4 on v3

--- a/solution.py
+++ b/solution.py
@@ -123,8 +123,9 @@
 
     w_sent = exchange(w_own, w_near, w_far, 0)
     v_sent = exchange(v_one, v_near, v_far, 2)
-    p_sent = [exchange(*(ref.at[at_row[c]:at_row[c] + sent[c]] for ref in (pc_own, pc_near, pc_far)), 4 + 2 * c)
-              for c in range(parts)]
+    pieces = ((0, 48), (48, sent[0]))
+    p_sent = [exchange(*(ref.at[a:b] for ref in (pc_own, pc_near, pc_far)), 4 + 2 * n)
+              for n, (a, b) in enumerate(pieces)]
     w_up = pltpu.make_async_remote_copy(
         src_ref=w_own, dst_ref=w_held, send_sem=send_sem.at[8], recv_sem=recv_sem.at[8],
         device_id=bridge_id, device_id_type=MESH)
@@ -135,13 +136,12 @@
     def await_barrier():
         pl.semaphore_wait(barrier, 1 + has_far.astype(jnp.int32) + tails.astype(jnp.int32))
 
-    def send_basis():
-        for copies in p_sent:
-            @pl.when(jnp.logical_not(heads))
-            def start_now():
-                launch_far(copies)
-
-            copies[1].start()
+    def send_basis(piece):
+        @pl.when(jnp.logical_not(heads))
+        def start_now():
+            launch_far(p_sent[piece])
+
+        p_sent[piece][1].start()
 
     def send_vector():
         @pl.when(jnp.logical_not(heads))
@@ -169,6 +169,8 @@
         def announce():
             pl.semaphore_signal(met_sem, inc=1, device_id=bridge_id, device_id_type=MESH)
             pl.semaphore_signal(met_sem, inc=1, device_id=far_id, device_id_type=MESH)
+
+        send_basis(0)
 
     loads[1].wait()
     cell_row = lax.broadcasted_iota(jnp.int32, (cells, agg_count), 0)
@@ -194,7 +196,7 @@
     @pl.when(jnp.logical_not(lazy))
     def tell():
         send_vector()
-        send_basis()
+        send_basis(1)
 
     loads[3].wait()
     loads[4].wait()
@@ -366,7 +368,8 @@
         def meet_late():
             await_barrier()
             send_vector()
-            send_basis()
+            send_basis(0)
+            send_basis(1)
 
         @pl.when(bridges)
         def hand_on():
@@ -379,7 +382,8 @@
             for k in range(rest):
                 acc_s[at_row[c]:at_row[c] + tall[c], k * cells:(k + 1) * cells] = basis_part(oh_own, c, k)
         for c in range(parts):
-            p_sent[c][1].wait_recv()
+            for copies in p_sent:
+                copies[1].wait_recv()
             split_basis(pc_near, c)
             for k in range(rest):
                 acc_s[at_row[c]:at_row[c] + tall[c], k * cells:(k + 1) * cells] += basis_part(oh_near, c, k)
@@ -427,7 +431,8 @@
         lax.fori_loop(0, pairs_here * tiles, product_step, 0)
 
     for c in range(parts):
-        await_far(p_sent[c][0], pc_far.at[at_row[c]:at_row[c] + tall[c]])
+        for copies, (a, b) in zip(p_sent, pieces):
+            await_far(copies[0], pc_far.at[a:b])
         split_basis(pc_far, c)
         height = counts[c] * order
         for k in range(rest):

time: 19.6 us -> 18.7 us (0.954)
  Pallas kernels: 18.8 us -> 18 us
    pallas_call x1, Pallas kernels: 18 us -> 17.1 us  [body(): pl.pallas_call(functools.partial(kernel, n_fine, n_coarse), out_shape=(vm...]
where the time goes in v4:
time: 18.7 us; the launch traced here: 18.6 us
  Pallas kernels  18 us (96%)
  between operations  0.67 us (4%)
    pallas_call x1, Pallas kernels, body(): pl.pallas_call(functools.partial(kernel, n_fine, n_coarse), out_shape=(vm...  17.1 us
    pallas_call x1, Pallas kernels, body(): pl.pallas_call(functools.partial(finish, n_fine, n_coarse), out_shape=(ja...  0.82 us

profile of v4, /device:TPU:6, one launch (start us, length us, event | category | flops | bytes accessed | tf_op | source)
XLA Modules:
  0.0 18.6 jit_solution(7369705439650585968)
XLA Ops:
  0.6 0.0 copy-start
  0.6 0.0 copy-start.1
  0.7 17.1 %shard_map.104 = (f32[800,128]{1,0:T(8,128)S(1)}, f32[192,128]{1,0:T(8,128)S(1)}) custom-call(f32[10,10,7,512]{3,2,1,0:T(8,128)} %bitcast.3, s32[7,512]{1,0:T(8,128)} %col_hbm.1, s32[7,512]{1,0:T(8,128)} %slot_hbm.1, s32[6,128]{1,0:T(8,128)} %bitcast.4, f32[10,10,512]{2,1,0:T(8,128)} %p_hbm.1, s32[15,64]{1,0:T(8,128)} %mem_hbm.1, f32[10,64]{1,0:T(8,128)} %rhs_v.1, ...), custom_call_target="tpu_custom_call" | custom-call | tf_op jit(solution)/shard_map/pallas_call | solution.py:543
  17.8 0.0 copy-done
  17.8 0.0 copy-done.1
  17.8 0.8 %shard_map.105 = (f32[10,10,7,64]{3,2,1,0:T(8,128)}, f32[10,64]{1,0:T(8,128)}) custom-call(f32[800,128]{1,0:T(8,128)S(1)} %get-tuple-element.6.op_s, f32[192,128]{1,0:T(8,128)S(1)} %get-tuple-element.7.small_s, s32[7,64]{1,0:T(8,128)S(1)} %copy-done.1, f32[10,64]{1,0:T(8,128)S(1)} %copy-done), custom_call_target="tpu_custom_call" | custom-call | tf_op jit(solution)/shard_map/pallas_call | solution.py:553
Async XLA Ops:
  0.6 17.2 %copy-start = (f32[10,64]{1,0:T(8,128)S(1)}, f32[10,64]{1,0:T(8,128)}, u32[]{:S(2)}) copy-start(f32[10,64]{1,0:T(8,128)} %rhs_v.1) | copy-start | bytes 7684
  0.6 17.2 %copy-start.1 = (s32[7,64]{1,0:T(8,128)S(1)}, s32[7,64]{1,0:T(8,128)}, u32[]{:S(2)}) copy-start(s32[7,64]{1,0:T(8,128)} %cc_v.1) | copy-start | bytes 5380

commit v5 on v4

--- a/solution.py
+++ b/solution.py
@@ -154,6 +154,12 @@
 
         w_sent[1].start()
 
+    @pl.when(tails)
+    def announce():
+        await_barrier()
+        pl.semaphore_signal(met_sem, inc=1, device_id=bridge_id, device_id_type=MESH)
+        pl.semaphore_signal(met_sem, inc=1, device_id=far_id, device_id_type=MESH)
+
     loads[0].wait()
     pc_own[...] = jnp.zeros_like(pc_own)
     for c in range(parts):
@@ -163,12 +169,9 @@
 
     @pl.when(jnp.logical_not(lazy))
     def meet():
-        await_barrier()
-
-        @pl.when(tails)
-        def announce():
-            pl.semaphore_signal(met_sem, inc=1, device_id=bridge_id, device_id_type=MESH)
-            pl.semaphore_signal(met_sem, inc=1, device_id=far_id, device_id_type=MESH)
+        @pl.when(jnp.logical_not(tails))
+        def meet_now():
+            await_barrier()
 
         send_basis(0)
 
@@ -179,24 +182,28 @@
         hit = cell_row == mem_v[place:place + 1, :]
         found = hit if found is None else jnp.logical_or(found, hit)
     mt_s[...] = jnp.where(found, 1.0, 0.0).astype(BF16)
+
+    loads[2].wait()
+    v_pad[...] = jnp.zeros_like(v_pad)
+    v_pad[0:order, :] = guess_v[...]
+    high, low = halves(v_pad[...])
+    whl_s[0:16, 0:agg_count] = high
+    whl_s[16:32, 0:agg_count] = low
+    both = dot_nt(whl_s[:, 0:agg_count], mt_s[...])
+    v_cells = both[0:order, :] + both[16:16 + order, :]
+    w_own[...] = jnp.zeros_like(w_own)
+    for j in range(order):
+        w_own[j:j + 1, :] = jnp.sum(p_v[j] * v_cells, axis=0, keepdims=True)
+
+    @pl.when(jnp.logical_not(lazy))
+    def tell():
+        send_vector()
+        send_basis(1)
+
     eye = jnp.where(
         lax.broadcasted_iota(jnp.int32, (agg_count, agg_count), 0)
         == lax.broadcasted_iota(jnp.int32, (agg_count, agg_count), 1), 1.0, 0.0).astype(BF16)
     m_s[...] = dot_nt(eye, mt_s[...]).astype(BF16)
-
-    loads[2].wait()
-    v_pad[...] = jnp.zeros_like(v_pad)
-    v_pad[0:order, :] = guess_v[...]
-    high, low = halves(v_pad[...])
-    v_cells = (dot_nn(high, m_s[...]) + dot_nn(low, m_s[...]))[0:order, :]
-    w_own[...] = jnp.zeros_like(w_own)
-    for j in range(order):
-        w_own[j:j + 1, :] = jnp.sum(p_v[j] * v_cells, axis=0, keepdims=True)
-
-    @pl.when(jnp.logical_not(lazy))
-    def tell():
-        send_vector()
-        send_basis(1)
 
     loads[3].wait()
     loads[4].wait()
@@ -411,8 +418,11 @@
         pairs_here = counts[c] // 2
 
         def product_step(step, carry):
-            pair = step // tiles
-            t = lax.rem(step, tiles)
+            product_tile(step // (tiles // 2), lax.rem(step, tiles // 2) * 2)
+            product_tile(step // (tiles // 2), lax.rem(step, tiles // 2) * 2 + 1)
+            return carry
+
+        def product_tile(pair, t):
             lanes = pl.ds(pl.multiple_of(t * LANES, LANES), LANES)
             base = t * span + pair * 16
             taken = [[g_s[pl.ds(pl.multiple_of(base + (j * counts[c] + ll) * 8, 8), fine_rows), :]
@@ -426,9 +436,7 @@
                         total[ll] = term if total[ll] is None else total[ll] + term
                 for ll in range(2):
                     prod_s[pl.ds(pl.multiple_of(base + (i * counts[c] + ll) * 8, 8), fine_rows), :] = total[ll]
-            return carry
-
-        lax.fori_loop(0, pairs_here * tiles, product_step, 0)
+        lax.fori_loop(0, pairs_here * tiles // 2, product_step, 0)
 
     for c in range(parts):
         for copies, (a, b) in zip(p_sent, pieces):

time: 18.7 us -> 18.6 us (level)
  Pallas kernels: 18 us -> 17.8 us
where the time goes in v5:
time: 18.6 us; the launch traced here: 18.5 us
  Pallas kernels  17.8 us (96%)
  between operations  0.67 us (4%)
    pallas_call x1, Pallas kernels, body(): pl.pallas_call(functools.partial(kernel, n_fine, n_coarse), out_shape=(vm...  17 us
    pallas_call x1, Pallas kernels, body(): pl.pallas_call(functools.partial(finish, n_fine, n_coarse), out_shape=(ja...  0.82 us

profile of v5, /device:TPU:6, one launch (start us, length us, event | category | flops | bytes accessed | tf_op | source)
XLA Modules:
  0.0 18.5 jit_solution(8562515221584280321)
XLA Ops:
  0.6 0.0 copy-start
  0.6 0.0 copy-start.1
  0.7 17.0 %shard_map.104 = (f32[800,128]{1,0:T(8,128)S(1)}, f32[192,128]{1,0:T(8,128)S(1)}) custom-call(f32[10,10,7,512]{3,2,1,0:T(8,128)} %bitcast.3, s32[7,512]{1,0:T(8,128)} %col_hbm.1, s32[7,512]{1,0:T(8,128)} %slot_hbm.1, s32[6,128]{1,0:T(8,128)} %bitcast.4, f32[10,10,512]{2,1,0:T(8,128)} %p_hbm.1, s32[15,64]{1,0:T(8,128)} %mem_hbm.1, f32[10,64]{1,0:T(8,128)} %rhs_v.1, ...), custom_call_target="tpu_custom_call" | custom-call | tf_op jit(solution)/shard_map/pallas_call | solution.py:551
  17.7 0.0 copy-done
  17.7 0.0 copy-done.1
  17.7 0.8 %shard_map.105 = (f32[10,10,7,64]{3,2,1,0:T(8,128)}, f32[10,64]{1,0:T(8,128)}) custom-call(f32[800,128]{1,0:T(8,128)S(1)} %get-tuple-element.6.op_s, f32[192,128]{1,0:T(8,128)S(1)} %get-tuple-element.7.small_s, s32[7,64]{1,0:T(8,128)S(1)} %copy-done.1, f32[10,64]{1,0:T(8,128)S(1)} %copy-done), custom_call_target="tpu_custom_call" | custom-call | tf_op jit(solution)/shard_map/pallas_call | solution.py:561
Async XLA Ops:
  0.6 17.0 %copy-start = (f32[10,64]{1,0:T(8,128)S(1)}, f32[10,64]{1,0:T(8,128)}, u32[]{:S(2)}) copy-start(f32[10,64]{1,0:T(8,128)} %rhs_v.1) | copy-start | bytes 7684
  0.6 17.0 %copy-start.1 = (s32[7,64]{1,0:T(8,128)S(1)}, s32[7,64]{1,0:T(8,128)}, u32[]{:S(2)}) copy-start(s32[7,64]{1,0:T(8,128)} %cc_v.1) | copy-start | bytes 5380

commit v6 on v5

--- a/solution.py
+++ b/solution.py
@@ -353,10 +353,9 @@
                 picked = wide_line == jnp.full((agg_count, cells), s, BF16)
                 rt_s[(s - 1) * agg_count:s * agg_count, k * cells:(k + 1) * cells] = jnp.where(picked, member, none)
 
-        def q_step(step, carry):
-            pair = step // tiles
-
-            lanes = pl.ds(pl.multiple_of(lax.rem(step, tiles) * LANES, LANES), LANES)
+        def q_tile(pair, t):
+
+            lanes = pl.ds(pl.multiple_of(t * LANES, LANES), LANES)
             blocks = [[a_v[r, pair * 2 + jj, :, lanes] for r in range(order)] for jj in range(2)]
             for i in range(order):
                 total = [None, None]
@@ -367,9 +366,13 @@
                         total[jj] = term if total[jj] is None else total[jj] + term
                 for jj in range(2):
                     q_s[i, pair * 2 + jj, :, lanes] = total[jj]
+
+        def q_step(step, carry):
+            for half in range(2):
+                q_tile(step // (tiles // 2), lax.rem(step, tiles // 2) * 2 + half)
             return carry
 
-        lax.fori_loop(0, order // 2 * tiles, q_step, 0)
+        lax.fori_loop(0, order // 2 * tiles // 2, q_step, 0)
 
         @pl.when(lazy)
         def meet_late():
@@ -418,8 +421,8 @@
         pairs_here = counts[c] // 2
 
         def product_step(step, carry):
-            product_tile(step // (tiles // 2), lax.rem(step, tiles // 2) * 2)
-            product_tile(step // (tiles // 2), lax.rem(step, tiles // 2) * 2 + 1)
+            for t in range(tiles):
+                product_tile(step, t)
             return carry
 
         def product_tile(pair, t):
@@ -436,7 +439,7 @@
                         total[ll] = term if total[ll] is None else total[ll] + term
                 for ll in range(2):
                     prod_s[pl.ds(pl.multiple_of(base + (i * counts[c] + ll) * 8, 8), fine_rows), :] = total[ll]
-        lax.fori_loop(0, pairs_here * tiles // 2, product_step, 0)
+        lax.fori_loop(0, pairs_here, product_step, 0)
 
     for c in range(parts):
         for copies, (a, b) in zip(p_sent, pieces):

time: 18.6 us -> 18.5 us (level)
  no operation moved by 1% of the time
where the time goes in v6:
time: 18.5 us; the launch traced here: 18.4 us
  Pallas kernels  17.7 us (96%)
  between operations  0.67 us (4%)
    pallas_call x1, Pallas kernels, body(): pl.pallas_call(functools.partial(kernel, n_fine, n_coarse), out_shape=(vm...  16.9 us
    pallas_call x1, Pallas kernels, body(): pl.pallas_call(functools.partial(finish, n_fine, n_coarse), out_shape=(ja...  0.82 us

profile of v6, /device:TPU:6, one launch (start us, length us, event | category | flops | bytes accessed | tf_op | source)
XLA Modules:
  0.0 18.4 jit_solution(1391008359508979015)
XLA Ops:
  0.6 0.0 copy-start
  0.6 0.0 copy-start.1
  0.7 16.9 %shard_map.104 = (f32[800,128]{1,0:T(8,128)S(1)}, f32[192,128]{1,0:T(8,128)S(1)}) custom-call(f32[10,10,7,512]{3,2,1,0:T(8,128)} %bitcast.3, s32[7,512]{1,0:T(8,128)} %col_hbm.1, s32[7,512]{1,0:T(8,128)} %slot_hbm.1, s32[6,128]{1,0:T(8,128)} %bitcast.4, f32[10,10,512]{2,1,0:T(8,128)} %p_hbm.1, s32[15,64]{1,0:T(8,128)} %mem_hbm.1, f32[10,64]{1,0:T(8,128)} %rhs_v.1, ...), custom_call_target="tpu_custom_call" | custom-call | tf_op jit(solution)/shard_map/pallas_call | solution.py:554
  17.5 0.0 copy-done
  17.5 0.0 copy-done.1
  17.6 0.8 %shard_map.105 = (f32[10,10,7,64]{3,2,1,0:T(8,128)}, f32[10,64]{1,0:T(8,128)}) custom-call(f32[800,128]{1,0:T(8,128)S(1)} %get-tuple-element.6.op_s, f32[192,128]{1,0:T(8,128)S(1)} %get-tuple-element.7.small_s, s32[7,64]{1,0:T(8,128)S(1)} %copy-done.1, f32[10,64]{1,0:T(8,128)S(1)} %copy-done), custom_call_target="tpu_custom_call" | custom-call | tf_op jit(solution)/shard_map/pallas_call | solution.py:564
Async XLA Ops:
  0.6 16.9 %copy-start = (f32[10,64]{1,0:T(8,128)S(1)}, f32[10,64]{1,0:T(8,128)}, u32[]{:S(2)}) copy-start(f32[10,64]{1,0:T(8,128)} %rhs_v.1) | copy-start | bytes 7684
  0.6 16.9 %copy-start.1 = (s32[7,64]{1,0:T(8,128)S(1)}, s32[7,64]{1,0:T(8,128)}, u32[]{:S(2)}) copy-start(s32[7,64]{1,0:T(8,128)} %cc_v.1) | copy-start | bytes 5380
